TPU v7x, 32 devices: a whole 2x2x4 slice. The times are simulated.
32 devices in a mesh: pts: 8 (over z, y), blk: 4 (over x, core).
Axes of the slice: x: 2, y: 2, z: 4, core: 2. Of those that a mesh axis runs over, the one named last changes fastest.
Arguments:
- points: bfloat16 [16384, 512], P('pts', 'blk'), may hold values from -6 to 6
- neighbours: int32 [16384, 27], P('pts'), may hold values from 0 to 16383, as said below
- patch_ids: int32 [16384], P('pts'), may hold values from 0 to 31, as said below
- conv_weight: bfloat16 [27, 512, 512], P(None, 'blk'), may hold values from -0.0546875 to 0.0546875
- conv_bias: float32 [512], P('blk'), may hold values from -3 to 3
- cpe_weight: bfloat16 [512, 512], P('blk'), may hold values from -0.25 to 0.25
- cpe_bias: float32 [512], P('blk'), may hold values from -3 to 3
- cpe_gain: float32 [512], P('blk'), may hold values from 0.1 to 1.9
- cpe_shift: float32 [512], P('blk'), may hold values from -1.75 to 1.75
- first_gain: float32 [512], P('blk'), may hold values from 0.1 to 1.9
- first_shift: float32 [512], P('blk'), may hold values from -1.75 to 1.75
- qkv_weight: bfloat16 [512, 3, 512], P(None, None, 'blk'), may hold values from -0.25 to 0.25
- query_value_bias: float32 [2, 512], P(None, 'blk'), may hold values from -3 to 3
- proj_weight: bfloat16 [512, 512], P('blk'), may hold values from -4 to 4
- proj_bias: float32 [512], P('blk'), may hold values from -3 to 3
- second_gain: float32 [512], P('blk'), may hold values from 0.1 to 1.9
- second_shift: float32 [512], P('blk'), may hold values from -1.75 to 1.75
- hidden_weight: bfloat16 [512, 2048], P(None, 'blk'), may hold values from -0.25 to 0.25
- hidden_bias: float32 [2048], P('blk'), may hold values from -3 to 3
- output_weight: bfloat16 [2048, 512], P('blk'), may hold values from -0.125 to 0.125
- output_bias: float32 [512], P('blk'), may hold values from -3 to 3
- out_grad: bfloat16 [16384, 512], P('pts', 'blk'), may hold values from -8 to 8
Outputs:
- block_out: bfloat16 [16384, 512], P('pts', 'blk')
- grad_points: float32 [16384, 512], P('pts', 'blk')
- grad_conv_weight: float32 [27, 512, 512], P(None, 'blk', 'pts')
- grad_conv_bias: float32 [512], P('blk')
- grad_cpe_weight: float32 [512, 512], P('blk', 'pts')
- grad_cpe_bias: float32 [512], P('blk')
- grad_cpe_gain: float32 [512], P('blk')
- grad_cpe_shift: float32 [512], P('blk')
- grad_first_gain: float32 [512], P('blk')
- grad_first_shift: float32 [512], P('blk')
- grad_qkv_weight: float32 [512, 3, 512], P('pts', None, 'blk')
- grad_query_value_bias: float32 [2, 512], P(None, 'blk')
- grad_proj_weight: float32 [512, 512], P('blk', 'pts')
- grad_proj_bias: float32 [512], P('blk')
- grad_second_gain: float32 [512], P('blk')
- grad_second_shift: float32 [512], P('blk')
- grad_hidden_weight: float32 [512, 2048], P('pts', 'blk')
- grad_hidden_bias: float32 [2048], P('blk')
- grad_output_weight: float32 [2048, 512], P('blk', 'pts')
- grad_output_bias: float32 [512], P('blk')
Inputs may be any that keep to these rules, and one draw needn't show every extreme that they name: Each neighbour lies at most 256 positions from its own point; in every draw some neighbours lie exactly 256 positions before and after their point. `patch_ids`: patch ids never fall along the points; each patch lies inside one aligned block of 1024 points and holds 1 to 1024 points, some exactly 1024; patches of different indices of pts have different ids.
All inputs are finite; a program needn't handle non-finite values.
Results may differ from a plain program's by a relative error of at most 0.02.
Values may be sent and summed in bfloat16 or wider, within the bound.
No kernel may reach another device: no remote copies, remote signals or barrier semaphores. Data moves between devices by JAX's collectives and lax.ppermute only.
A program may use at most 256 MiB of HBM per device.

v0:
```python
import functools
import math

import jax
import jax.numpy as jnp
from jax import lax
from jax.experimental import pallas as pl
from jax.experimental.pallas import tpu as pltpu
from jax.sharding import PartitionSpec as P

HEAD_DIM = 16
PATCH = 1024
KERNEL = 27
REACH = 256
EPS = 1e-05
LOG2E = math.log2(math.e)
BF = jnp.bfloat16
F32 = jnp.float32
NN = ((1,), (0,))
NT = ((1,), (1,))
TN = ((0,), (0,))
VMEM = pl.BlockSpec(memory_space=pltpu.VMEM)
SMEM = pl.BlockSpec(memory_space=pltpu.SMEM)
HBM = pl.BlockSpec(memory_space=pltpu.HBM)
ANY = pl.BlockSpec(memory_space=pl.ANY)
TILE = 256


def dot(a, b, dims):
    return lax.dot_general(a, b, (dims, ((), ())), preferred_element_type=F32)


def struct(shape, kind):
    return jax.ShapeDtypeStruct(shape, kind)


TIMES = {
    "prepare": 10,  "conv_forward": 7.5, "first_rows": 2.5, "triple_half": 2, "attend_forward": 21, "second_rows": 10,
    "second_send": 1.5, "attend_backward": 19, "second_keep": 2.5, "layer_grad": 1, "third_rows": 2.3, "cpe_weights": 0.1,
    "spread": 7, "third_weights": 0.1, "conv_weight_grad": 0.1, "finish": 1.0, "rows_out": 2.0, "fold": 0.05, "second_out": 0.1, "grads_out": 0.1,
}
FACTOR = 0.3
TINY = 0.1
BLOCK = 4.2


def call(name, kernel, inputs, outputs, scratch=(), mib=8, grid=None, first=(), time=None):
    count, extra = len(inputs), len(first)

    def body(*refs):
        kernel(*refs[:count], *refs[count + extra :])

    options = {} if grid is None else {"grid": grid}
    result = pl.pallas_call(
        body,
        out_shape=[o for o, spec in outputs],
        in_specs=[spec for a, spec in inputs] + [ANY] * extra,
        out_specs=[spec for o, spec in outputs],
        scratch_shapes=list(scratch),
        compiler_params=pltpu.CompilerParams(vmem_limit_bytes=mib * 2**20),
        cost_estimate=pl.CostEstimate(flops=int((time or TIMES[name]) * FACTOR * 1.15e9), bytes_accessed=0, transcendentals=0),
        name=name,
        **options,
    )(*[pltpu.with_memory_space_constraint(a, pltpu.HBM) if spec is HBM else a for a, spec in inputs], *first)
    return result[0] if len(result) == 1 else result


def vm(*arrays):
    return [(a, VMEM) for a in arrays]


def split3(values):
    high = values.astype(BF)
    rest = values - high.astype(F32)
    middle = rest.astype(BF)
    return high, middle, (rest - middle.astype(F32)).astype(BF)


def joined(rows, width):
    rows = rows.astype(F32)
    return (rows[:, :width] + rows[:, width : 2 * width]) + rows[:, 2 * width : 3 * width]


def in_order(pieces, me):
    core, chip = (me & 1) == 1, (me >> 1) == 1
    a, b = jnp.where(core, pieces[1], pieces[0]), jnp.where(core, pieces[0], pieces[1])
    c, d = jnp.where(core, pieces[3], pieces[2]), jnp.where(core, pieces[2], pieces[3])
    return [
        jnp.where(chip, c, a),
        jnp.where(chip, d, b),
        jnp.where(chip, a, c),
        jnp.where(chip, b, d),
    ]


def folded(source, start, target, row, sems, rows):
    part, width = rows // 4, source.shape[1]
    copies = []
    for j in range(4):
        copies.append(
            pltpu.make_async_copy(
                source.at[pl.ds(pl.multiple_of(start + j * part, 16), part), :],
                target.at[row : row + part, j * width : (j + 1) * width],
                sems(),
            )
        )
    return copies


def unfolded(pack, row, at, rows):
    part, width = rows // 4, pack.shape[1] // 4
    return jnp.concatenate(
        [
            pack[row : row + part, j * width : (j + 1) * width]
            for j in range(at.start // part, at.stop // part)
        ],
        axis=0,
    )


class Plan:
    def __init__(self, rows, width):
        fold = rows // 4
        self.first_cpe = 3 * width
        self.first_points = 4 * width
        self.first_small = 4 * width + 2 * fold
        self.first_rows = self.first_small + 16
        self.near_points = width
        self.near_small = width + fold
        self.near_rows = self.near_small + 16


def counter(sems):
    state = [0]

    def take():
        state[0] += 1
        return sems.at[state[0] - 1]

    return take


VECTORS = 10


def prepare_kernel(
    plan, rows, place_of, turned_in, cpe, points, patch, *refs
):
    vectors, refs = refs[:VECTORS], refs[VECTORS:]
    hidden_bias, query_bias, away, near, turned, small, patch_row, terms, lines, long_line, pair, straight, sems = refs
    me = place_of[0]
    width = points.shape[1]
    take = counter(sems)
    copies = [
        pltpu.make_async_copy(cpe, away.at[plan.first_cpe : plan.first_cpe + width, :], take()),
        pltpu.make_async_copy(cpe, near.at[0:width, :], take()),
    ]
    for e in (2, 3):
        copies += folded(points, (me ^ e) * rows, away, plan.first_points + (e - 2) * rows // 4, take, rows)
    copies += folded(points, (me ^ 1) * rows, near, plan.near_points, take, rows)
    straight_copy = pltpu.make_async_copy(turned_in, straight, take())
    straight_copy.start()
    for copy in copies:
        copy.start()
    loads = [pltpu.make_async_copy(vector, lines.at[r], take()) for r, vector in enumerate(vectors)]
    loads.append(pltpu.make_async_copy(hidden_bias, long_line, take()))
    loads.append(pltpu.make_async_copy(query_bias, pair, take()))
    for copy in loads:
        copy.start()
    for e in (0, 1):
        at = pl.ds(pl.multiple_of((me ^ e) * rows, rows), rows)
        loads.append(pltpu.make_async_copy(patch.at[:, at], patch_row.at[:, e * rows : (e + 1) * rows], take()))
        loads[-1].start()
    straight_copy.wait()
    for t in range(3):
        turned[t * width : (t + 1) * width, :] = straight[t].T
    for copy in loads:
        copy.wait()
    for r in range(VECTORS):
        small[r : r + 1, :] = lines[r]
    for i in range(4):
        small[VECTORS + i : VECTORS + i + 1, :] = long_line[:, i * width : (i + 1) * width]
    small[VECTORS + 4 :, :] = pair[...]
    high, middle, low = split3(small[...])
    terms[...] = jnp.concatenate([high, middle, low, jnp.zeros_like(low)], axis=1)
    last = [
        pltpu.make_async_copy(turned, away.at[0 : 3 * width, :], take()),
        pltpu.make_async_copy(terms, away.at[plan.first_small :, :], take()),
        pltpu.make_async_copy(terms, near.at[plan.near_small :, :], take()),
    ]
    for copy in last:
        copy.start()
    for copy in copies + last:
        copy.wait()


def prepare(plan, place_of, turned, cpe, points, patch, vectors, hidden_bias, query_bias, first=()):
    row_count, width = points.shape
    wide = cpe.shape[1]
    lines = [v.reshape(1, -1) for v in (*vectors, hidden_bias)]
    return call(
        "prepare",
        functools.partial(prepare_kernel, plan, row_count // 4),
        [(place_of, SMEM), (turned, HBM), (cpe, HBM), (points, HBM), (patch.reshape(1, -1), HBM)]
        + [(v, HBM) for v in (*lines, query_bias)],
        [
            (struct((plan.first_rows, wide), BF), HBM),
            (struct((plan.near_rows, wide), BF), HBM),
            (struct((3 * width, wide), BF), VMEM),
            (struct((16, width), F32), VMEM),
            (struct((1, row_count // 2), jnp.int32), VMEM),
        ],
        [
            pltpu.VMEM((16, wide), BF),
            pltpu.VMEM((VECTORS, 1, width), F32),
            pltpu.VMEM((1, 4 * width), F32),
            pltpu.VMEM((2, width), F32),
            pltpu.VMEM(turned.shape, BF),
            pltpu.SemaphoreType.DMA((17 + VECTORS + 5,)),
        ],
        first=first,
    )


def one_hot(place):
    spots = lax.broadcasted_iota(jnp.int32, (256, 256), 0).astype(F32).astype(BF)
    place = jnp.broadcast_to(place.astype(F32).astype(BF), (256, 256))
    return jnp.where(spots == place, jnp.ones((), BF), jnp.zeros((), BF))


def conv_kernel(e, packs, place_of, low, points, high, lookup, weight, *refs):
    sources, refs = refs[:packs], refs[packs:]
    conv, conv_after, gathered = refs[:3]
    away, near = refs[3:5] if packs else (None, None)
    turned, picked, sems = refs[-3:]
    me = place_of[0]
    width = points.shape[1]
    rows = picked.shape[1]
    quarter = me ^ e
    take = counter(sems)
    copies = []
    if packs:
        hidden, output, proj, upstream = sources
        wide, fold = hidden.shape[1], rows // 4
        start = 2 * wide + width
        for target in (away, near):
            copies.append(pltpu.make_async_copy(output, target.at[0:wide, :], take()))
            copies.append(pltpu.make_async_copy(proj, target.at[wide : wide + width, :], take()))
            copies.append(pltpu.make_async_copy(hidden, target.at[wide + width : start, :], take()))
        copies += folded(upstream, (me ^ 2) * rows, away, start, take, rows)
        copies += folded(upstream, (me ^ 3) * rows, away, start + fold, take, rows)
        copies += folded(upstream, (me ^ 1) * rows, near, start, take, rows)
        at = slice(start + fold, start + 3 * fold)
        copies.append(pltpu.make_async_copy(output.at[: 2 * fold, :], near.at[at, :], take()))
        for copy in copies:
            copy.start()
    base = place_of[1] * points.shape[0] + quarter * rows - REACH
    last = points.shape[0] // 256 - 1
    for j in range(rows // 256 + 2):
        spot = quarter * (rows // 256) - 1 + j
        at = pl.multiple_of(jnp.clip(spot, 0, last) * 256, 256)
        piece = points[pl.ds(at, 256), :]
        piece = jnp.where(spot < 0, low[...], jnp.where(spot > last, high[...], piece))
        turned[j * width : (j + 1) * width, :] = piece.T
    step = KERNEL // 3
    for b in range(rows // 256):
        cols = slice(b * 256, (b + 1) * 256)
        left = turned[b * width : (b + 3) * width, :]
        for k in range(KERNEL):
            spot = lookup[k : k + 1, pl.ds(pl.multiple_of(quarter * rows + b * 256, 256), 256)] - base
            part = jnp.broadcast_to(lax.shift_right_logical(spot, 8) - b, (width, 256))
            three = dot(left, one_hot(jnp.bitwise_and(spot, 255)), NN)
            values = jnp.where(
                part == 0,
                three[:width],
                jnp.where(part == 1, three[width : 2 * width], three[2 * width :]),
            )
            picked[k * width : (k + 1) * width, cols] = values.astype(BF)
            if k % step == step - 1:
                at = slice((k + 1 - step) * width, (k + 1) * width)
                copies.append(pltpu.make_async_copy(picked.at[at, cols], gathered.at[at, cols], take()))
                copies[-1].start()
        (conv, conv_after)[b][...] = dot(picked[:, cols], weight[...], TN).astype(conv.dtype)
    for copy in copies:
        copy.wait()


def conv_forward(e, place_of, low, points, high, lookup, weight, kind, packs=(), first=(), time=None):
    rows, width, wide = points.shape[0] // 4, points.shape[1], weight.shape[1]
    outputs = [(struct((rows // 2, wide), kind), VMEM)] * 2 + [(struct((KERNEL * width, rows), BF), HBM)]
    if packs:
        size = 2 * wide + width + rows // 4
        outputs += [(struct((size + rows // 4, wide), BF), HBM), (struct((size + rows // 2, wide), BF), HBM)]
    return call(
        "conv_forward",
        functools.partial(conv_kernel, e, len(packs)),
        [(place_of, SMEM)] + vm(low, points, high, lookup, weight) + [(p, HBM) for p in packs],
        outputs,
        [
            pltpu.VMEM(((rows // 256 + 2) * width, 256), BF),
            pltpu.VMEM((KERNEL * width, rows), BF),
            pltpu.SemaphoreType.DMA((6 * rows // 512 + (19 if packs else 0),)),
        ],
        first=first,
        time=time,
    )


def spread_kernel(e, blocks, place_of, lookup, weight, grads, out, upstream):
    width = out.shape[0]
    rows = grads.shape[0]
    quarter = place_of[0] ^ e
    base = place_of[1] * lookup.shape[1] + quarter * rows - REACH
    out[...] = jnp.zeros(out.shape, F32)
    step = 9
    for n, b in enumerate(blocks):
        cols = slice(b * 256, (b + 1) * 256)
        upstream[...] = dot(weight[...], grads[cols, :], NT)
        for s in range(KERNEL // step):
            left, right = [], []
            for k in range(s * step, (s + 1) * step):
                spot = lookup[k : k + 1, pl.ds(pl.multiple_of(quarter * rows + b * 256, 256), 256)] - base
                part = jnp.broadcast_to(lax.shift_right_logical(spot, 8) - b, (width, 256))
                mine = upstream[k * width : (k + 1) * width, :]
                left.append(
                    jnp.concatenate(
                        [jnp.where(part == i, mine, 0.0).astype(BF) for i in range(3)], axis=0
                    )
                )
                right.append(one_hot(jnp.bitwise_and(spot, 255)))
            three = dot(jnp.concatenate(left, axis=1), jnp.concatenate(right, axis=1), NT)
            for i in range(3):
                at = slice((n + i) * 256, (n + i + 1) * 256)
                out[:, at] = out[:, at] + three[i * width : (i + 1) * width]


def spread(e, blocks, place_of, lookup, weight, grads, first=(), time=None):
    width = weight.shape[0] // KERNEL
    return call(
        "spread",
        functools.partial(spread_kernel, e, blocks),
        [(place_of, SMEM)] + vm(lookup, weight, grads),
        [(struct((width, 256 * len(blocks) + 2 * REACH), F32), VMEM)],
        [pltpu.VMEM((KERNEL * width, 256), F32)],
        first=first,
        time=time,
    )


def halves(count, stage):
    keep = [r for r in range(count) if not (r >> stage) & 1]
    return keep, [r ^ (1 << stage) for r in keep]


def conv_weight_kernel(blocks, stage, start, count, extra, place_of, *refs):
    gathered, grads, refs = refs[:4], refs[4:8], refs[8:]
    thirds, (mine, theirs, total) = refs[:extra], refs[extra:]
    tile = 384
    for i in range(count // tile):
        rows = slice(start + i * tile, start + (i + 1) * tile)
        cols = slice(i * tile, (i + 1) * tile)
        total[:, cols] = sum(dot(a[rows, :], g[...], NN) for a, g in zip(gathered, grads)).T.astype(BF)
    size = total.shape[0] // blocks
    for out, slots in zip((mine, theirs), halves(blocks, stage)):
        for i, r in enumerate(slots):
            at = pl.multiple_of((place_of[1] ^ r) * size, size)
            out[i, :, 0:count] = total[pl.ds(at, size), :]
            if extra:
                out[i, :, count:] = (thirds[0][r].astype(F32) + thirds[1][r].astype(F32)).astype(BF)


def conv_weight_grad(place_of, gathered, grads, start, count, blocks, stage, thirds=(), first=()):
    wide = grads[0].shape[1]
    cols = count + (thirds[0].shape[2] if thirds else 0)
    half = struct((blocks // 2, wide // blocks, cols), BF)
    return call(
        "conv_weight_grad",
        functools.partial(conv_weight_kernel, blocks, stage, start, count, len(thirds)),
        [(place_of, SMEM)] + vm(*gathered, *grads, *thirds),
        vm(half, half),
        [pltpu.VMEM((wide, count), BF)],
        first=first,
    )


def finish_kernel(place_of, s0, s1, s2, s2_after, s3, s3_after, out, low, high):
    me = place_of[0]
    rows = s0.shape[1] - 2 * REACH
    ends = [s[:, 0:256] for s in (s0, s1, s2, s3)], [s[:, 768:] for s in (s0, s1)] + [s[:, 512:] for s in (s2_after, s3_after)]
    inner = [
        [s[:, 256:512] for s in (s0, s1)]
        + [a[:, 256:512] + b[:, 0:256] for a, b in ((s2, s2_after), (s3, s3_after))],
        [s[:, 512:768] for s in (s0, s1)]
        + [a[:, 512:768] + b[:, 256:512] for a, b in ((s2, s2_after), (s3, s3_after))],
    ]
    parts = [in_order(p, me) for p in (ends[0], inner[0], inner[1], ends[1])]
    out[...] = jnp.zeros(out.shape, F32)
    for q in range(4):
        for i, part in enumerate(parts):
            at = slice(q * rows + i * 256, q * rows + (i + 1) * 256)
            out[:, at] = out[:, at] + part[q]
    low[...] = out[:, :REACH].astype(BF)
    high[...] = out[:, out.shape[1] - REACH :].astype(BF)


def finish(place_of, spreads, first=()):
    width, span = spreads[0].shape
    total = 4 * (span - 2 * REACH) + 2 * REACH
    return call(
        "finish",
        finish_kernel,
        [(place_of, SMEM)] + vm(*spreads),
        [(struct((width, total), F32), VMEM)] + [(struct((width, REACH), BF), VMEM)] * 2,
        first=first,
    )


def rows_out_kernel(place_of, inside, below, above, block, own, near, far, cross, block_out, out):
    rows, width = own.shape
    me = place_of[0]
    pieces = in_order([block[...], near[:, :width], far[:, :width], cross[:, width : 2 * width]], me)
    for q in range(4):
        block_out[q * rows : (q + 1) * rows, :] = pieces[q]
    pieces = [own[...], near[:, width:], far[:, 2 * width : 3 * width], cross[:, 3 * width :]]
    pieces = in_order(pieces, me)
    for q in range(4):
        total = inside[:, REACH + q * rows : REACH + (q + 1) * rows].T + pieces[q].astype(F32)
        out[q * rows : (q + 1) * rows, :] = total
    out[:REACH, :] = out[:REACH, :] + below[...].astype(F32).T
    last = out.shape[0] - REACH
    out[last:, :] = out[last:, :] + above[...].astype(F32).T


def rows_out(place_of, inside, below, above, block, own, near, far, cross, first=()):
    rows, width = own.shape
    return call(
        "rows_out",
        rows_out_kernel,
        [(place_of, SMEM)] + vm(inside, below, above, block, own, near, far, cross),
        vm(struct((4 * rows, width), BF), struct((4 * rows, width), F32)),
        first=first,
    )


def three_rows(high, middle, low):
    spots = lax.broadcasted_iota(jnp.int32, (16, high.shape[1]), 0)
    picked = jnp.where(
        spots == 0,
        high.astype(F32),
        jnp.where(spots == 1, middle.astype(F32), jnp.where(spots == 2, low.astype(F32), 0.0)),
    )
    return picked.astype(BF)


def one_rows(length, count):
    spots = lax.broadcasted_iota(jnp.int32, (16, length), 0)
    return jnp.where(spots < count, 1.0, 0.0).astype(BF)


def patch_codes(patch):
    shape = (32, patch.shape[1])
    spots = lax.broadcasted_iota(jnp.int32, shape, 0)
    bits = jnp.bitwise_and(
        lax.shift_right_logical(jnp.broadcast_to(patch, shape), jnp.bitwise_and(spots, 15)), 1
    )
    bits = jnp.where(spots < 16, bits, 1 - bits)
    return jnp.where(bits == 1, 1.0, 0.0).astype(BF), jnp.where(bits == 1, 0.0, -1e30).astype(BF)


def fixed_rows(patch, query_side, key_side):
    length = patch.shape[1]
    left, right = patch_codes(patch)
    key_side[48:64, :] = one_rows(length, 3)
    key_side[64:96, :] = left
    query_side[64:96, :] = right
    key_side[96:128, :] = jnp.zeros((32, length), BF)
    query_side[96:128, :] = jnp.zeros((32, length), BF)


def column(row):
    return jnp.broadcast_to(row, (128, 128)).T[:, 0:1]


def triple_rows(values, weights, smalls, out, cols):
    width = out.shape[1] // 2
    for t in range(3):
        for i in range(2):
            piece = dot(weights[i][t * width : (t + 1) * width, :], values, NT)
            if t != 1:
                piece = piece + column(smalls[i][14 + t // 2 : 15 + t // 2, :])
            out[t, i * width : (i + 1) * width, cols] = piece.astype(BF)


def triple_half_kernel(plan, values, turned, away, small, out):
    smalls = (small[...], joined(away[plan.first_small :, :], small.shape[1]))
    triple_rows(values[...], (turned, away), smalls, out, slice(0, values.shape[0]))


def triple_half(plan, values, turned, away, small):
    return call(
        "triple_half",
        functools.partial(triple_half_kernel, plan),
        vm(values, turned, away, small),
        [(struct((3, 2 * small.shape[1], values.shape[0]), BF), VMEM)],
    )


def attend_forward_kernel(
    plan, heads, tile, mine, other, turned, away, small, patch, triple, total, keep, send, logs, query_side, key_side, value_side
):
    rows = mine.shape[2]
    length = 2 * rows
    for t in range(3):
        triple[t, :, :rows] = mine[t]
    smalls = (small[...], joined(away[plan.first_small :, :], small.shape[1]))
    triple_rows(other[...], (turned, away), smalls, triple, slice(rows, length))
    fixed_rows(patch[...], query_side, key_side)
    value_side[16:32, :] = one_rows(length, 1)

    @pl.loop(0, heads)
    def _(h):
        at = pl.ds(pl.multiple_of(h * HEAD_DIM, HEAD_DIM), HEAD_DIM)
        query = triple[0, at, :].astype(F32) * (HEAD_DIM**-0.5 * LOG2E)
        key = triple[1, at, :]
        high, middle, low = split3(query)
        query_side[0:16, :] = high
        query_side[16:32, :] = middle
        query_side[32:48, :] = low
        query_side[48:64, :] = jnp.zeros((16, length), BF)
        key_side[0:16, :] = key
        key_side[16:32, :] = key
        key_side[32:48, :] = key
        value_side[0:16, :] = triple[2, at, :]
        wide_key = key.astype(F32)
        bound = jnp.max(jnp.sum(query * query, axis=0)) * jnp.max(
            jnp.sum(wide_key * wide_key, axis=0)
        )
        logs[pl.ds(h, 1), :] = jnp.zeros((1, length), F32)

        @pl.when(jnp.logical_not(bound < 4096.0))
        def _():
            for t in range(length // tile):
                cols = slice(t * tile, (t + 1) * tile)
                top = jnp.max(dot(key_side[...], query_side[:, cols], TN), axis=0, keepdims=True)
                query_side[48:64, cols] = three_rows(*split3(-top))
                logs[pl.ds(h, 1), cols] = top

        for t in range(length // tile):
            cols = slice(t * tile, (t + 1) * tile)
            weights = jnp.exp2(dot(key_side[...], query_side[:, cols], TN)).astype(BF)
            mixed = dot(value_side[...], weights, NN)
            sums = mixed[16:17, :]
            mixed = mixed[0:16, :] * (1.0 / sums)
            total[at, cols] = mixed
            if t * tile < rows:
                keep[at, cols] = mixed.astype(BF)
            else:
                send[at, t * tile - rows : (t + 1) * tile - rows] = mixed.astype(BF)
            logs[pl.ds(h, 1), cols] = logs[pl.ds(h, 1), cols] + jnp.log2(sums)


def attend_forward(plan, mine, other, turned, away, small, patch, first=()):
    width, rows = mine.shape[1:]
    length = 2 * rows
    heads = width // HEAD_DIM
    return call(
        "attend_forward",
        functools.partial(attend_forward_kernel, plan, heads, 512),
        vm(mine, other, turned, away, small, patch),
        [
            (struct((3, width, length), BF), VMEM),
            (struct((width, length), F32), VMEM),
            (struct((width, rows), BF), VMEM),
            (struct((width, rows), BF), VMEM),
            (struct((heads, length), F32), VMEM),
        ],
        [
            pltpu.VMEM((128, length), BF),
            pltpu.VMEM((128, length), BF),
            pltpu.VMEM((32, length), BF),
        ],
        first=first,
    )


def attend_backward_kernel(
    first, heads, tile, triple, patch, mine, other, mixed, logs, out, query_side, key_side, value_side, grad_side, grad_value, grad_key
):
    length = triple.shape[2]
    fixed_rows(patch[...], query_side, key_side)
    value_side[16:32, :] = one_rows(length, 3)

    @pl.loop(0, heads)
    def _(h):
        at = pl.ds(pl.multiple_of((h + first) * HEAD_DIM, HEAD_DIM), HEAD_DIM)
        to = pl.ds(pl.multiple_of(h * HEAD_DIM, HEAD_DIM), HEAD_DIM)
        query, key = triple[0, at, :], triple[1, at, :]
        upstream = jnp.concatenate([mine[at, :], other[at, :]], axis=1)
        high, middle, low = split3(query.astype(F32) * (HEAD_DIM**-0.5 * LOG2E))
        query_side[0:16, :] = high
        query_side[16:32, :] = middle
        query_side[32:48, :] = low
        query_side[48:64, :] = three_rows(*split3(-logs[pl.ds(h + first, 1), :]))
        key_side[0:16, :] = key
        key_side[16:32, :] = key
        key_side[32:48, :] = key
        value_side[0:16, :] = triple[2, at, :]
        inner = jnp.sum(upstream.astype(F32) * mixed[at, :], axis=0, keepdims=True)
        grad_side[0:16, :] = upstream
        grad_side[16:32, :] = three_rows(*split3(-inner))
        for t in range(length // tile):
            cols = slice(t * tile, (t + 1) * tile)
            prob = jnp.exp2(dot(query_side[:, cols], key_side[...], TN))
            grad_prob = dot(grad_side[:, cols], value_side[...], TN)
            grad_score = (prob * grad_prob).astype(BF)
            value_part = dot(upstream[:, cols], prob.astype(BF), NN)
            key_part = dot(query[:, cols], grad_score, NN)
            out[0, to, cols] = (dot(key, grad_score, NT) * HEAD_DIM**-0.5).astype(BF)
            if t == 0:
                grad_value[...] = value_part
                grad_key[...] = key_part
            else:
                grad_value[...] += value_part
                grad_key[...] += key_part
        out[1, to, :] = (grad_key[...] * HEAD_DIM**-0.5).astype(BF)
        out[2, to, :] = grad_value[...].astype(BF)


def attend_backward(first_head, heads, triple, patch, mine, other, mixed, logs, first=()):
    length = triple.shape[2]
    return call(
        "attend_backward",
        functools.partial(attend_backward_kernel, first_head, heads, 512),
        vm(triple, patch, mine, other, mixed, logs),
        [(struct((3, heads * HEAD_DIM, length), BF), VMEM)],
        [
            pltpu.VMEM((128, length), BF),
            pltpu.VMEM((128, length), BF),
            pltpu.VMEM((32, length), BF),
            pltpu.VMEM((32, length), BF),
            pltpu.VMEM((16, length), F32),
            pltpu.VMEM((16, length), F32),
        ],
        mib=12,
        first=first,
    )


def norm_rows(values):
    average = jnp.mean(values, axis=1, keepdims=True)
    scaling = lax.rsqrt(
        jnp.mean(values * values, axis=1, keepdims=True) - average * average + EPS
    )
    return (values - average) * scaling, scaling


def norm_rows_back(upstream, normed, scaling, gain):
    scaled = upstream * gain
    return scaling * (
        scaled
        - jnp.mean(scaled, axis=1, keepdims=True)
        - normed * jnp.mean(scaled * normed, axis=1, keepdims=True)
    )


def cut(values):
    width = values.shape[1] // 4
    return [values[:, j * width : (j + 1) * width] for j in range(4)]


def add_rows(ref, row, values, first):
    total = jnp.sum(values, axis=0, keepdims=True)
    ref[row : row + 1, :] = total if first else ref[row : row + 1, :] + total


def small_vectors(plan, small, near, far, cross):
    width = small.shape[1]
    return [
        small[...],
        joined(near[plan.near_small :, :], width),
        joined(far[plan.first_small :, :], width),
        joined(cross[plan.first_small :, :], width),
    ]


def vectors(smalls, me):
    return jnp.concatenate(in_order(smalls, me), axis=1)


def cpe_rows(plan, weight, near, far, cross, me):
    width = weight.shape[0]
    at = slice(plan.first_cpe, plan.first_cpe + width)
    pieces = [weight[...], near[:width, :], far[at, :], cross[at, :]]
    return jnp.concatenate(in_order(pieces, me), axis=0)


def own_rows(ref, me, rows, at):
    return ref[pl.ds(pl.multiple_of(me * rows + at.start, at.stop - at.start), at.stop - at.start), :]


def first_rows_kernel(
    plan, place_of, part_low, part_high, close_low, close_high, away, points, small, weight, near, far, cross,
    layer, middle, normed_cpe, scaling_cpe, residual, normed, scaling,
):
    me = place_of[0]
    rows = 2 * part_low.shape[0]
    vec = vectors(small_vectors(plan, small, near, far, cross), me)
    vec = [vec[r : r + 1, :] for r in range(6)]
    weights = cpe_rows(plan, weight, near, far, cross, me)
    for t in range(rows // TILE):
        at = slice(t * TILE, (t + 1) * TILE)
        part, close = ((part_low, close_low), (part_high, close_high))[t * TILE * 2 // rows]
        low = (part[...] + close[...].astype(F32) + away[at, :].astype(F32) + vec[0]).astype(BF)
        middle[at, :] = low
        xhat, rate = norm_rows(dot(low, weights, NN) + vec[1])
        normed_cpe[at, :] = xhat
        scaling_cpe[at, :] = rate
        features = [
            own_rows(points, me, rows, at),
            unfolded(near, plan.near_points, at, rows),
            unfolded(far, plan.first_points, at, rows),
            unfolded(cross, plan.first_points + rows // 4, at, rows),
        ]
        features = jnp.concatenate(in_order(features, me), axis=1)
        sums = features.astype(F32) + xhat * vec[2] + vec[3]
        residual[at, :] = sums
        xhat, rate = norm_rows(sums)
        normed[at, :] = xhat
        scaling[at, :] = rate
        layer[at, :] = (xhat * vec[4] + vec[5]).astype(BF)


def first_rows(plan, place_of, parts, closes, away, points, small, weight, near, far, cross):
    rows, wide = away.shape
    full, thin, lower = struct((rows, wide), F32), struct((rows, 1), F32), struct((rows, wide), BF)
    return call(
        "first_rows",
        functools.partial(first_rows_kernel, plan),
        [(place_of, SMEM)] + vm(*parts, *closes, away, points, small, weight, near, far, cross),
        vm(lower, lower, full, thin, full, full, thin),
    )


def gelu_parts(u):
    scale = math.sqrt(2 / math.pi)
    square = u * u
    bent = jnp.tanh(u * (scale + (scale * 0.044715) * square))
    half = 0.5 + 0.5 * bent
    slope = half + u * (1.0 - bent * bent) * (0.5 * scale + (1.5 * 0.044715 * scale) * square)
    return u * half, slope


def second_rows_kernel(
    plan, place_of, keep, got, residual, out_grad, hidden, output, proj, small, near, far, cross, near2, far2, cross2,
    block0, block1, block_far, active, before, layer, upstream, carried, low, grad_keep, grad_send, hidden_sums, sums,
):
    me = place_of[0]
    rows, wide = residual.shape
    smalls = small_vectors(plan, small, near, far, cross)
    vec = vectors(smalls, me)
    vec = {r: vec[r : r + 1, :] for r in (6, 7, 8, 9)}
    biases = [jnp.concatenate([s[10 + i : 11 + i, :] for i in range(4)], axis=1) for s in smalls]
    width = keep.shape[0] // 2
    packs = (near2, far2, cross2)
    end = wide + width
    hiddens = [hidden] + [p.at[end : end + wide, :] for p in packs]
    last = end + wide
    outputs = [output] + [p.at[0:wide, :] for p in packs]
    projs = [proj[...]] + [p[wide:end, :] for p in packs]
    mine = jnp.concatenate([projs[0], projs[2]], axis=0)
    others = jnp.concatenate([projs[1], projs[3]], axis=0)
    for t in range(rows // TILE):
        at = slice(t * TILE, (t + 1) * TILE)
        base = residual[at, :] + vec[6] + dot(keep[:, at], mine, TN) + dot(got[:, at], others, TN)
        normed, scaling = norm_rows(base)
        lower = (normed * vec[7] + vec[8]).astype(BF)
        layer[at, :] = lower
        grads = [
            own_rows(out_grad, me, rows, at),
            unfolded(near2, last, at, rows),
            unfolded(far2, last, at, rows),
            unfolded(cross2, last + rows // 4, at, rows),
        ]
        grads = jnp.concatenate(in_order(grads, me), axis=1)
        upstream[at, :] = grads
        result = base + vec[9]
        grad_layer = None
        for e in range(4):
            act, slope = gelu_parts(dot(lower, hiddens[e][...], NN) + biases[e])
            act = act.astype(BF)
            active[e, at, :] = act
            result = result + dot(act, outputs[e][...], NN)
            pre = dot(grads, outputs[e][...], NT) * slope
            add_rows(hidden_sums, e, pre, t == 0)
            pre = pre.astype(BF)
            before[e, at, :] = pre
            piece = dot(pre, hiddens[e][...], NT)
            grad_layer = piece if e == 0 else grad_layer + piece
        result = in_order(cut(result.astype(BF)), me)
        block0[at, :] = result[0]
        block1[at, :] = result[1]
        block_far[at, 0:width] = result[2]
        block_far[at, width:] = result[3]
        wide_grads = grads.astype(F32)
        add_rows(sums, 0, grad_layer * normed, t == 0)
        add_rows(sums, 1, grad_layer, t == 0)
        add_rows(sums, 3, wide_grads, t == 0)
        carry = wide_grads + norm_rows_back(grad_layer, normed, scaling, vec[7])
        carried[at, :] = carry
        add_rows(sums, 2, carry, t == 0)
        carry = carry.astype(BF)
        low[at, :] = carry
        grad_keep[:, at] = dot(mine, carry, NT).astype(BF)
        grad_send[:, at] = dot(others, carry, NT).astype(BF)


def second_rows(plan, place_of, keep, got, residual, out_grad, weights, small, firsts, seconds):
    rows, wide = residual.shape
    lower, piece = struct((rows, wide), BF), struct((rows, wide // 4), BF)
    heads = struct(keep.shape, BF)
    return call(
        "second_rows",
        functools.partial(second_rows_kernel, plan),
        [(place_of, SMEM)] + vm(keep, got, residual, out_grad, *weights, small, *firsts, *seconds),
        vm(
            piece,
            piece,
            struct((rows, wide // 2), BF),
            struct((4, rows, wide), BF),
            struct((4, rows, wide), BF),
            lower,
            lower,
            struct((rows, wide), F32),
            lower,
            heads,
            heads,
            struct((4, wide), F32),
            struct((4, wide), F32),
        ),
        mib=12,
    )


def cut_rows(store, spot, cols, value, blocks):
    size = value.shape[0] // blocks
    for p in range(blocks):
        store(p ^ spot, cols, value[p * size : (p + 1) * size])


def second_weight_parts(i, e, blocks, spot, upstream, active, before, layer, low, attended, store):
    wide = layer.shape[1]
    width = attended.shape[0] // 2
    cut_rows(store, spot, slice(0, wide), dot(layer[...], before[e], TN), blocks)
    cut_rows(store, spot, slice(wide, 2 * wide), dot(upstream[...], active[e], TN), blocks)
    part = dot(attended[i * width : (i + 1) * width, :], low[...], NN)
    cut_rows(store, spot, slice(2 * wide, 2 * wide + width), part.T, blocks)


def second_send_kernel(blocks, place_of, upstream, active, before, layer, low, attended, out):
    for i, e in enumerate((1, 3)):

        def store(p, cols, value):
            out[i, p, :, cols] = value.astype(BF)

        second_weight_parts(i, e, blocks, place_of[1], upstream, active, before, layer, low, attended, store)


def second_send(place_of, blocks, upstream, active, before, layer, low, attended):
    wide = layer.shape[1]
    return call(
        "second_send",
        functools.partial(second_send_kernel, blocks),
        [(place_of, SMEM)] + vm(upstream, active, before, layer, low, attended),
        [(struct((2, blocks, wide // blocks, 2 * wide + attended.shape[0] // 2), BF), VMEM)],
    )


def second_keep_kernel(blocks, place_of, upstream, active, before, layer, low, attended, got, mine, far):
    for i, out in enumerate((mine, far)):

        def store(p, cols, value):
            out[p, :, cols] = (value + got[i, p, :, cols].astype(F32)).astype(BF)

        second_weight_parts(i, 2 * i, blocks, place_of[1], upstream, active, before, layer, low, attended, store)


def second_keep(place_of, blocks, upstream, active, before, layer, low, attended, got, first=()):
    out = struct(got.shape[1:], BF)
    return call(
        "second_keep",
        functools.partial(second_keep_kernel, blocks),
        [(place_of, SMEM)] + vm(upstream, active, before, layer, low, attended, got),
        vm(out, out),
        first=first,
    )


def third_weights_kernel(
    blocks, place_of, first_half, second_half, mine, other, cpe_keep, cpe_got, small_keep, own, far
):
    rows = mine.shape[0]
    width = first_half.shape[1]
    size = own.shape[1]
    empty = jnp.zeros((size - 16, width), BF)
    for i, (grads, out) in enumerate(((first_half, own), (second_half, far))):

        def store(p, cols, value):
            out[p, :, cols] = value.astype(BF)

        for t in range(3):
            part = dot(grads[t, :, :rows], mine[...], NN) + dot(grads[t, :, rows:], other[...], NN)
            cut_rows(store, place_of[1], slice(t * width, (t + 1) * width), part.T, blocks)
        sums = [jnp.sum(grads[t].astype(F32).T, axis=0, keepdims=True) for t in (0, 2)]
        small_got = sum(cpe_got[i, slot, size:, :].astype(F32) for slot in range(3))
        small = small_keep[i] + small_got + jnp.concatenate([jnp.zeros((14, width), F32)] + sums, axis=0)
        for p in range(blocks):
            out[p, :, 3 * width : 4 * width] = (
                cpe_keep[i, p].astype(F32) + cpe_got[i, p, :size, :].astype(F32)
            ).astype(BF)
            out[p, 0:16, 4 * width :] = small.astype(BF)
            if empty.shape[0]:
                out[p, 16:, 4 * width :] = empty


def third_weights(place_of, blocks, first_half, second_half, mine, other, cpe_keep, cpe_got, small_keep, first=()):
    wide = mine.shape[1]
    width = first_half.shape[1]
    out = struct((blocks, wide // blocks, 5 * width), BF)
    return call(
        "third_weights",
        functools.partial(third_weights_kernel, blocks),
        [(place_of, SMEM)] + vm(first_half, second_half, mine, other, cpe_keep, cpe_got, small_keep),
        vm(out, out),
        first=first,
    )


def layer_grad_kernel(half, first_half, second_half, turned, away, out):
    width = first_half.shape[1]
    rows = first_half.shape[2] // 2
    cols = slice(half * rows, (half + 1) * rows)
    total = None
    for t in range(3):
        at = slice(t * width, (t + 1) * width)
        for grads, weight in ((first_half, turned), (second_half, away)):
            piece = dot(grads[t, :, cols], weight[at, :], TN)
            total = piece if total is None else total + piece
    out[...] = total.astype(out.dtype)


def layer_grad(half, first_half, second_half, turned, away, kind, first=()):
    return call(
        "layer_grad",
        functools.partial(layer_grad_kernel, half),
        vm(first_half, second_half, turned, away),
        [(struct((first_half.shape[2] // 2, turned.shape[1]), kind), VMEM)],
        first=first,
    )


def third_rows_kernel(
    plan, place_of, part, close, carried, normed, scaling, normed_cpe, scaling_cpe, small, weight, near, far, cross, block1, block_far,
    conv_grad, points0, near_rows, far_rows, low, sums,
):
    me = place_of[0]
    vec = vectors(small_vectors(plan, small, near, far, cross), me)
    weights = cpe_rows(plan, weight, near, far, cross, me)
    width = points0.shape[1]
    for t in range(part.shape[0] // TILE):
        at = slice(t * TILE, (t + 1) * TILE)
        upstream = part[at, :] + close[at, :].astype(F32)
        xhat = normed[at, :]
        add_rows(sums, 4, upstream * xhat, t == 0)
        add_rows(sums, 5, upstream, t == 0)
        grads = carried[at, :] + norm_rows_back(upstream, xhat, scaling[at, :], vec[4:5, :])
        pieces = in_order(cut(grads.astype(BF)), me)
        points0[at, :] = pieces[0]
        near_rows[at, 0:width] = block1[at, :]
        near_rows[at, width:] = pieces[1]
        far_rows[at, 0 : 2 * width] = block_far[at, :]
        far_rows[at, 2 * width : 3 * width] = pieces[2]
        far_rows[at, 3 * width :] = pieces[3]
        xhat = normed_cpe[at, :]
        add_rows(sums, 2, grads * xhat, t == 0)
        add_rows(sums, 3, grads, t == 0)
        grads = norm_rows_back(grads, xhat, scaling_cpe[at, :], vec[2:3, :])
        add_rows(sums, 1, grads, t == 0)
        lower = grads.astype(BF)
        low[at, :] = lower
        result = dot(lower, weights, NT)
        add_rows(sums, 0, result, t == 0)
        conv_grad[at, :] = result.astype(BF)


def third_rows(plan, place_of, part, close, carried, normed, scaling, normed_cpe, scaling_cpe, small, weight, firsts, blocks):
    rows, wide = part.shape
    lower, piece = struct((rows, wide), BF), struct((rows, wide // 4), BF)
    return call(
        "third_rows",
        functools.partial(third_rows_kernel, plan),
        [(place_of, SMEM)]
        + vm(part, close, carried, normed, scaling, normed_cpe, scaling_cpe, small, weight, *firsts, *blocks),
        vm(lower, piece, struct((rows, wide // 2), BF), lower, lower, struct((6, wide), F32)),
    )


def cpe_weights_kernel(
    blocks, place_of, middle, low, sums_one, sums_two, hidden_sums, send, keep, small_keep, small_send
):
    me = place_of[0]
    width = middle.shape[1] // 4
    ones, twos = in_order(cut(sums_one[...]), me), in_order(cut(sums_two[...]), me)
    for e in range(4):
        out = (keep, send, keep, send)[e]

        def store(p, cols, value):
            out[e // 2, p, : value.shape[0], cols] = value.astype(BF)

        at = pl.ds(pl.multiple_of((e ^ me) * width, width), width)
        cut_rows(store, place_of[1], slice(0, width), dot(low[...], middle[:, at], TN), blocks)
        out = (small_keep, small_send, small_keep, small_send)[e]
        out[e // 2, 0:6, :] = ones[e]
        out[e // 2, 6:10, :] = twos[e]
        for i in range(4):
            out[e // 2, 10 + i : 11 + i, :] = hidden_sums[e : e + 1, i * width : (i + 1) * width]
        out[e // 2, 14:16, :] = jnp.zeros((2, width), F32)
    size = send.shape[2] - 16
    for i in range(2):
        for slot, term in enumerate(split3(small_send[i])):
            send[i, slot, size:, :] = term
        send[i, 3:, size:, :] = jnp.zeros((blocks - 3, 16, width), BF)


def cpe_weights(blocks, place_of, middle, low, sums_one, sums_two, hidden_sums, first=()):
    wide = middle.shape[1]
    send = struct((2, blocks, wide // blocks + 16, wide // 4), BF)
    keep = struct((2, blocks, wide // blocks, wide // 4), BF)
    small = (2, 16, wide // 4)
    return call(
        "cpe_weights",
        functools.partial(cpe_weights_kernel, blocks),
        [(place_of, SMEM)] + vm(middle, low, sums_one, sums_two, hidden_sums),
        vm(send, keep, struct(small, F32)),
        [pltpu.VMEM(small, F32)],
        first=first,
    )


def fold_kernel(keep, send, mine, got, kept, sent):
    for out, slots in ((sent, send), (kept, keep)):
        for i, j in enumerate(slots):
            out[i] = (mine[j].astype(F32) + got[j].astype(F32)).astype(BF)


def fold(mine, got, keep, send, first=()):
    out = struct((len(keep), *mine.shape[1:]), BF)
    return call("fold", functools.partial(fold_kernel, keep, send), vm(mine, got), vm(out, out), first=first)


def second_out_kernel(mine, got, hidden, output, proj):
    total = mine[0].astype(F32) + got[0].astype(F32)
    wide = hidden.shape[1]
    hidden[...] = total[:, :wide]
    output[...] = total[:, wide : 2 * wide]
    proj[...] = total[:, 2 * wide :]


def second_out(mine, got, wide):
    size, cols = mine.shape[1:]
    return call(
        "second_out",
        second_out_kernel,
        vm(mine, got),
        vm(struct((size, wide), F32), struct((size, wide), F32), struct((size, cols - 2 * wide), F32)),
    )


def grads_out_kernel(chunk, m0, g0, m1, g1, m2, g2, conv, cpe, qkv, *lines):
    width = cpe.shape[1]
    for i, (mine, got) in enumerate(((m0, g0), (m1, g1), (m2, g2))):
        part = mine[0, :, :chunk].astype(F32) + got[0, :, :chunk].astype(F32)
        for k in range(chunk // width):
            conv[i * (chunk // width) + k] = part[:, k * width : (k + 1) * width]
    third = m1[0, :, chunk:].astype(F32) + g1[0, :, chunk:].astype(F32)
    for t in range(3):
        qkv[t] = third[:, t * width : (t + 1) * width]
    cpe[...] = third[:, 3 * width : 4 * width]
    small = third[:16, 4 * width :]
    for r in range(VECTORS):
        lines[r][...] = small[r : r + 1, :]
    for i in range(4):
        lines[VECTORS][:, i * width : (i + 1) * width] = small[VECTORS + i : VECTORS + i + 1, :]
    lines[VECTORS + 1][...] = small[VECTORS + 4 :, :]


def grads_out(sums, chunk, width):
    size = sums[0].mine.shape[1]
    line = struct((1, width), F32)
    return call(
        "grads_out",
        functools.partial(grads_out_kernel, chunk),
        vm(*[a for s in sums for a in (s.mine, s.got)]),
        vm(struct((KERNEL, size, width), F32), struct((size, width), F32), struct((3, size, width), F32))
        + vm(*[line] * VECTORS, struct((1, 4 * width), F32), struct((2, width), F32)),
    )


def swap(values, e, axis="blk"):
    return lax.ppermute(values, axis, [(i, i ^ e) for i in range(lax.axis_size(axis))])


def after(values, *first):
    return lax.optimization_barrier((values, *first))[0]


def total_of(first, second):
    return (first.astype(F32) + second.astype(F32)).astype(BF)


class Scatter:
    def __init__(self, mine, theirs, count, stage):
        self.mine, self.theirs = mine, theirs
        self.numbers, _ = halves(count, stage)
        self.order = [stage] + [b for b in range(count.bit_length() - 1) if b != stage]
        self.got = swap(theirs, 1 << stage, "pts")

    def advance(self, *first):
        bit = self.order[1]
        keep = [j for j, r in enumerate(self.numbers) if not (r >> bit) & 1]
        send = [self.numbers.index(self.numbers[j] ^ (1 << bit)) for j in keep]
        self.mine, self.theirs = fold(self.mine, self.got, keep, send, first)
        self.numbers = [self.numbers[j] for j in keep]
        self.order = self.order[1:]
        self.got = swap(self.theirs, 1 << bit, "pts")
        return self.theirs

    def finish(self):
        while len(self.order) > 1:
            self.advance()
        return self


def shards(
    points, neighbours, patch_ids, conv_weight, conv_bias, cpe_weight, cpe_bias, cpe_gain, cpe_shift, first_gain,
    first_shift, qkv_weight, query_value_bias, proj_weight, proj_bias, second_gain, second_shift, hidden_weight,
    hidden_bias, output_weight, output_bias, out_grad,
):
    row_count, width = points.shape
    wide = conv_weight.shape[2]
    mine = row_count // 4
    shard_count = lax.axis_size("pts")
    me = lax.axis_index("blk")
    place_of = jnp.stack([me, lax.axis_index("pts")]).astype(jnp.int32)
    plan = Plan(mine, width)
    ups = [(i, i + 1) for i in range(shard_count - 1)]
    downs = [(i + 1, i) for i in range(shard_count - 1)]

    low = lax.ppermute(points[row_count - REACH :], "pts", ups)
    high = lax.ppermute(points[:REACH], "pts", downs)
    kernel_rows = conv_weight.reshape(KERNEL * width, wide)
    lookup = neighbours.T
    away_pack, near_pack, turned, small, patch_row = prepare(
        plan,
        place_of,
        qkv_weight.transpose(1, 0, 2),
        cpe_weight,
        points,
        patch_ids,
        (conv_bias, cpe_bias, cpe_gain, cpe_shift, first_gain, first_shift, proj_bias, second_gain, second_shift, output_bias),
        hidden_bias,
        query_value_bias,
        first=(low,),
    )
    far = swap(away_pack, 2)
    near = swap(near_pack, 1)

    *part3, gathered3, away_pack, near_pack = conv_forward(
        3, place_of, low, points, high, lookup, kernel_rows, BF, (hidden_weight, output_weight, proj_weight, out_grad),
    )
    got3 = [swap(p, 1) for p in part3]
    *part2, gathered2 = conv_forward(2, place_of, low, points, high, lookup, kernel_rows, BF, first=(part3[0],))
    far_part = swap(jnp.concatenate([total_of(a, b) for a, b in zip(part2, got3)], axis=0), 2)
    *part1, gathered1 = conv_forward(1, place_of, low, points, high, lookup, kernel_rows, BF, first=(part2[0],))
    *part0, gathered0 = conv_forward(0, place_of, low, points, high, lookup, kernel_rows, F32, first=(part1[0],), time=0.5)
    cross = swap(after(far, part2[0]), 1)
    close_part = [swap(p, 1) for p in part1]
    firsts = (near, far, cross)
    layer_one, conv_low, normed_cpe, scaling_cpe, residual_one, normed_one, scaling_one = first_rows(
        plan, place_of, part0, close_part, far_part, points, small, cpe_weight, *firsts
    )
    other_one = swap(layer_one, 1)
    far2 = swap(after(away_pack, part1[0]), 2)
    near2 = swap(near_pack, 1)


    half = triple_half(plan, layer_one, turned, far, small)
    triple, mixed, keep, send, logs = attend_forward(plan, half, other_one, turned, far, small, patch_row)
    got = swap(send, 1)
    cross2 = swap(after(far2, send), 1)
    (
        block0, block1, block_far, active, before, layer_two, upstream, carried, carried_low, grad_keep, grad_send,
        sum_hidden_bias, sums_two,
    ) = second_rows(
        plan, place_of, keep, got, residual_one, out_grad, (hidden_weight, output_weight, proj_weight), small, firsts,
        (near2, far2, cross2),
    )
    grad_got = swap(grad_send, 1)

    weights_send = second_send(place_of, shard_count, upstream, active, before, layer_two, carried_low, got)
    weights_got = swap(after(weights_send, grad_got), 1)
    heads = width // HEAD_DIM
    grad_first = attend_backward(
        0, heads, triple, patch_row, grad_keep, grad_got, mixed, logs, first=(weights_send,)
    )
    weights_mine, weights_far = second_keep(
        place_of, shard_count, upstream, active, before, layer_two, carried_low, keep, weights_got, first=(grad_first,)
    )
    weights_far = swap(weights_far, 2)
    grad_second = attend_backward(
        heads, heads, triple, patch_row, grad_keep, grad_got, mixed, logs, first=(weights_mine,)
    )
    layer_send = layer_grad(1, grad_first, grad_second, turned, far, BF)
    layer_got = swap(layer_send, 1)
    layer_part = layer_grad(0, grad_first, grad_second, turned, far, F32, first=(layer_send,))
    conv_grad, points0, near_rows, far_rows, cpe_low, sums_one = third_rows(
        plan, place_of, layer_part, layer_got, carried, normed_one, scaling_one, normed_cpe, scaling_cpe, small, cpe_weight, firsts, (block1, block_far)
    )
    grad0 = conv_grad
    grad2 = swap(grad0, 2)
    grad1 = swap(grad0, 1)
    second_mine, second_theirs = fold(weights_mine, weights_far, *halves(shard_count, 0))
    second = Scatter(second_mine, second_theirs, shard_count, 0)
    spread0 = spread(0, (0, 1), place_of, lookup, kernel_rows, grad0, first=(weights_far,), time=TINY)
    cpe_send, cpe_keep, small_keep = cpe_weights(
        shard_count, place_of, conv_low, cpe_low, sums_one, sums_two, sum_hidden_bias, first=(spread0,)
    )
    cpe_got = swap(cpe_send, 1)
    third_mine, third_far = third_weights(
        place_of, shard_count, grad_first, grad_second, layer_one, other_one, cpe_keep, cpe_got, small_keep,
        first=(spread0, grad2, second.got),
    )
    grad3 = swap(after(grad2, cpe_send), 1)

    gathered = (gathered0, gathered1, gathered2, gathered3)
    grads = (grad0, grad1, grad2, grad3)
    chunk = KERNEL // 3 * width
    third_far = swap(after(third_far, grad2), 2)
    piece0, theirs0 = conv_weight_grad(
        place_of, gathered, grads, 0, chunk, shard_count, 0, first=(third_mine,)
    )
    sum0 = Scatter(piece0, theirs0, shard_count, 0)
    second_sent = second.advance(piece0)
    spread1 = spread(1, (0, 1), place_of, lookup, kernel_rows, grad1, first=(piece0, second_sent), time=TINY)
    piece1, theirs1 = conv_weight_grad(
        place_of, gathered, grads, chunk, chunk, shard_count, 0, thirds=(third_mine, third_far), first=(spread1,)
    )
    sum1 = Scatter(piece1, theirs1, shard_count, 0)
    sent = sum0.advance(piece1)
    piece2, theirs2 = conv_weight_grad(
        place_of, gathered, grads, 2 * chunk, chunk, shard_count, 0, first=(piece1, sent)
    )
    sum2 = Scatter(piece2, theirs2, shard_count, 0)
    spread2 = spread(2, (0,), place_of, lookup, kernel_rows, grad2, first=(piece2,), time=BLOCK)
    far_rows = swap(after(far_rows, piece2), 2)
    near_rows = swap(after(near_rows, piece2), 1)
    sent = sum0.advance(spread2)
    second_sent = second.advance(spread2)
    spread2_after = spread(2, (1,), place_of, lookup, kernel_rows, grad2, first=(spread2, sent, second_sent), time=BLOCK)
    spread3 = spread(3, (0,), place_of, lookup, kernel_rows, grad3, first=(spread2_after,), time=BLOCK)
    sent = sum1.advance(spread3)
    spread3_after = spread(3, (1,), place_of, lookup, kernel_rows, grad3, first=(spread3, sent, sum0.got, second.got), time=BLOCK)

    sent = sum2.advance(spread3_after)
    second = second.finish()
    grad_hidden, grad_output, grad_proj = second_out(second.mine, second.got, wide)
    grad_padded, to_below, to_above = finish(
        place_of, (spread0, spread1, spread2, spread2_after, spread3, spread3_after), first=(sent, grad_hidden)
    )
    cross_rows = swap(after(far_rows, spread3), 1)
    from_above = lax.ppermute(to_below, "pts", downs)
    from_below = lax.ppermute(to_above, "pts", ups)
    sent = sum1.advance(grad_padded)
    sent = sum2.advance(sent)
    block_out, grad_points = rows_out(
        place_of, grad_padded, from_below, from_above, block0, points0, near_rows, far_rows, cross_rows,
        first=(sent,),
    )

    grad_conv, grad_cpe, grad_qkv, *lines = grads_out([s.finish() for s in (sum0, sum1, sum2)], chunk, width)
    small = [line.reshape(-1) for line in lines[: VECTORS + 1]]
    return (
        block_out,
        grad_points,
        grad_conv.transpose(0, 2, 1),
        small[0],
        grad_cpe.T,
        *small[1:6],
        grad_qkv.transpose(1, 0, 2),
        lines[VECTORS + 1],
        grad_proj.T,
        small[8],
        small[6],
        small[7],
        grad_hidden,
        small[10],
        grad_output.T,
        small[9],
    )


def solution(mesh):
    return jax.shard_map(
        shards,
        mesh=mesh,
        in_specs=(
            P("pts", "blk"),
            P("pts", None),
            P("pts"),
            P(None, "blk", None),
            P("blk"),
            P("blk", None),
            P("blk"),
            P("blk"),
            P("blk"),
            P("blk"),
            P("blk"),
            P(None, None, "blk"),
            P(None, "blk"),
            P("blk", None),
            P("blk"),
            P("blk"),
            P("blk"),
            P(None, "blk"),
            P("blk"),
            P("blk", None),
            P("blk"),
            P("pts", "blk"),
        ),
        out_specs=(
            P("pts", "blk"),
            P("pts", "blk"),
            P(None, "blk", "pts"),
            P("blk"),
            P("blk", "pts"),
            P("blk"),
            P("blk"),
            P("blk"),
            P("blk"),
            P("blk"),
            P("pts", None, "blk"),
            P(None, "blk"),
            P("blk", "pts"),
            P("blk"),
            P("blk"),
            P("blk"),
            P("pts", "blk"),
            P("blk"),
            P("blk", "pts"),
            P("blk"),
        ),
        check_vma=False,
    )
```

profile of v0, /device:TPU:5, one launch (start us, length us, event | category | flops | bytes accessed | tf_op | source)
XLA Modules:
  0.0 247.9 jit_solution(5480168295218342224)
XLA Ops:
  1.5 1.9 collective-permute-start.1
  3.5 4.3 %collective-permute-start = (bf16[256,128]{1,0:T(8,128)(2,1)S(1)}, bf16[256,128]{1,0:T(8,128)(2,1)S(1)}, u32[]{:S(2)}, u32[]{:S(2)}) collective-permute-start(bf16[256,128]{1,0:T(8,128)(2,1)S(1)} %get-tuple-element.247), channel_id=1, source_target_pairs={{0,4},{4,8},{8,12},{12,16},{16,20},{20,24},{24,28},{1,5},{5,9},{9,... | collective-permute-start | bytes 196616 | tf_op jit(solution)/shard_map/ppermute | solution.py:1158
  7.8 1.9 collective-permute-done.refs_1_.refs_17_
  9.7 2.6 %prepare.1 = (bf16[784,512]{1,0:T(8,128)(2,1)S(1)}, bf16[272,512]{1,0:T(8,128)(2,1)S(1)}, bf16[384,512]{1,0:T(8,128)(2,1)S(1)}, f32[16,128]{1,0:T(8,128)S(1)}, s32[1,1024]{1,0:T(1,128)S(1)}) custom-call(s32[2]{0:T(128)S(1)} %pad_add_fusion.refs_0_, bf16[3,512,128]{2,1,0:T(8,128)(2,1)} %bitcast.54, bf16[128,512]{1,0:T(8,128)(2,1)} %refs_9_.3, ...), custom_call_target="tpu_custom_call" | custom-call | flops 3449999872 | tf_op jit(solution)/shard_map/prepare/pallas_call | solution.py:54
  13.2 7.4 %conv_forward.4 = (bf16[256,512]{1,0:T(8,128)(2,1)S(1)}, bf16[256,512]{1,0:T(8,128)(2,1)S(1)}, bf16[3456,512]{1,0:T(8,128)(2,1)S(1)}, bf16[1408,512]{1,0:T(8,128)(2,1)S(1)}, bf16[1536,512]{1,0:T(8,128)(2,1)S(1)}) custom-call(s32[2]{0:T(128)S(1)} %pad_add_fusion.refs_0_, bf16[256,128]{1,0:T(8,128)(2,1)S(1)} %collective-permute-done.refs_1_.refs_17_, ...), custom_call_target="tpu_custom_call" | custom-call | flops 2587500032 | tf_op jit(solution)/shard_map/conv_forward/pallas_call | solution.py:54
  20.6 1.9 collective-permute-start.4
  22.6 7.4 %conv_forward.5 = (bf16[256,512]{1,0:T(8,128)(2,1)S(1)}, bf16[256,512]{1,0:T(8,128)(2,1)S(1)}, bf16[3456,512]{1,0:T(8,128)(2,1)S(1)}) custom-call(s32[2]{0:T(128)S(1)} %pad_add_fusion.refs_0_, bf16[256,128]{1,0:T(8,128)(2,1)S(1)} %collective-permute-done.refs_1_.refs_17_, bf16[2048,128]{1,0:T(8,128)(2,1)S(1)} %copy-done.2, ...), custom_call_target="tpu_custom_call" | custom-call | flops 2587500032 | tf_op jit(solution)/shard_map/conv_forward/pallas_call | solution.py:54
  30.6 2.1 collective-permute-start.9
  33.6 7.2 %conv_forward.6 = (bf16[256,512]{1,0:T(8,128)(2,1)S(1)}, bf16[256,512]{1,0:T(8,128)(2,1)S(1)}, bf16[3456,512]{1,0:T(8,128)(2,1)S(1)}) custom-call(s32[2]{0:T(128)S(1)} %pad_add_fusion.refs_0_, bf16[256,128]{1,0:T(8,128)(2,1)S(1)} %collective-permute-done.refs_1_.refs_17_, bf16[2048,128]{1,0:T(8,128)(2,1)S(1)} %copy-done.2, ...), custom_call_target="tpu_custom_call" | custom-call | flops 2587500032 | tf_op jit(solution)/shard_map/conv_forward/pallas_call | solution.py:54
  43.1 7.2 %conv_forward.7 = (f32[256,512]{1,0:T(8,128)S(1)}, f32[256,512]{1,0:T(8,128)S(1)}, bf16[3456,512]{1,0:T(8,128)(2,1)S(1)}) custom-call(s32[2]{0:T(128)S(1)} %pad_add_fusion.refs_0_, bf16[256,128]{1,0:T(8,128)(2,1)S(1)} %collective-permute-done.refs_1_.refs_17_, bf16[2048,128]{1,0:T(8,128)(2,1)S(1)} %copy-done.2, ...), custom_call_target="tpu_custom_call" | custom-call | flops 172500000 | tf_op jit(solution)/shard_map/conv_forward/pallas_call | solution.py:54
  50.3 1.7 first_rows.1
  52.8 1.2 triple_half.1.refs_0_
  54.3 30.9 %attend_forward.1 = (bf16[3,256,1024]{2,1,0:T(8,128)(2,1)S(1)}, f32[256,1024]{1,0:T(8,128)S(1)}, bf16[256,512]{1,0:T(8,128)(2,1)S(1)}, bf16[256,512]{1,0:T(8,128)(2,1)S(1)}, f32[16,1024]{1,0:T(8,128)S(1)}) custom-call(bf16[3,256,512]{2,1,0:T(8,128)(2,1)S(1)} %triple_half.1.refs_0_, bf16[512,512]{1,0:T(8,128)(2,1)S(1)} %collective-permute-done.10.refs_1_.refs_4_, ...), custom_call_target="tpu_custom_call" | custom-call | flops 7245000192 | tf_op jit(solution)/shard_map/attend_forward/pallas_call | solution.py:54
  85.7 3.1 %collective-permute-done.11.refs_2_.refs_6_ = bf16[256,512]{1,0:T(8,128)(2,1)S(1)} collective-permute-done((bf16[256,512]{1,0:T(8,128)(2,1)S(1)}, bf16[256,512]{1,0:T(8,128)(2,1)S(1)}, u32[]{:S(2)}, u32[]{:S(2)}) %collective-permute-start.11) | collective-permute-done | bytes 262176 | tf_op jit(solution)/shard_map/ppermute | solution.py:1109
  88.9 9.1 %second_rows.1 = (bf16[512,128]{1,0:T(8,128)(2,1)S(1)}, bf16[512,128]{1,0:T(8,128)(2,1)S(1)}, bf16[512,256]{1,0:T(8,128)(2,1)S(1)}, bf16[4,512,512]{2,1,0:T(8,12...) custom-call(s32[2]{0:T(128)S(1)} %pad_add_fusion.refs_0_, ...), custom_call_target="tpu_custom_call" | custom-call | flops 3449999872 | tf_op jit(solution)/shard_map/second_rows/pallas_call | solution.py:54
  98.5 2.1 second_send.1.refs_6_
  100.7 19.2 %attend_backward.2.refs_8_.refs_0_.refs_1_ = bf16[3,128,1024]{2,1,0:T(8,128)(2,1)S(1)} custom-call(bf16[3,256,1024]{2,1,0:T(8,128)(2,1)S(1)} %get-tuple-element.148.refs_0_, s32[1,1024]{1,0:T(1,128)S(1)} %get-tuple-element.147.refs_5_.refs_1_, bf16[256,512]{1,0:T(8,128)(2,1)S(1)} %get-tuple-element.156.refs_2_, ...), custom_call_target="tpu_custom_call" | custom-call | flops 6554999808 | tf_op jit(solution)/shard_map/attend_backward/pallas_call | solution.py:54
  119.9 2.1 second_keep.1
  122.9 19.6 %attend_backward.3.refs_1_.refs_2_ = bf16[3,128,1024]{2,1,0:T(8,128)(2,1)S(1)} custom-call(bf16[3,256,1024]{2,1,0:T(8,128)(2,1)S(1)} %get-tuple-element.148.refs_0_, s32[1,1024]{1,0:T(1,128)S(1)} %get-tuple-element.147.refs_5_.refs_1_, bf16[256,512]{1,0:T(8,128)(2,1)S(1)} %get-tuple-element.156.refs_2_, ...), custom_call_target="tpu_custom_call" | custom-call | flops 6554999808 | tf_op jit(solution)/shard_map/attend_backward/pallas_call | solution.py:54
  145.8 2.4 third_rows.1
  149.6 7.3 %spread.6.refs_6_.refs_8_.refs_1_ = f32[128,1024]{1,0:T(8,128)S(1)} custom-call(s32[2]{0:T(128)S(1)} %pad_add_fusion.refs_0_, s32[27,2048]{1,0:T(8,128)S(1)} %bitcast.47, bf16[3456,512]{1,0:T(8,128)(2,1)S(1)} %bitcast.37, bf16[512,512]{1,0:T(8,128)(2,1)S(1)} %get-tuple-element.174.refs_3_.refs_5_, ...), custom_call_target="tpu_custom_call" | custom-call | flops 34500000 | tf_op jit(solution)/shard_map/spread/pallas_call | solution.py:54
  156.9 1.3 cpe_weights.1
  158.3 1.3 collective-permute-start.22
  159.6 1.8 collective-permute-done.20.refs_9_.refs_7_.refs_3_
  161.4 1.2 collective-permute-start.21
  163.2 1.8 third_weights.1
  165.9 3.3 %conv_weight_grad.3 = (bf16[4,64,1152]{2,1,0:T(8,128)(2,1)S(1)}, bf16[4,64,1152]{2,1,0:T(8,128)(2,1)S(1)}) custom-call(s32[2]{0:T(128)S(1)} %pad_add_fusion.refs_0_, bf16[3456,512]{1,0:T(8,128)(2,1)S(1)} %get-tuple-element.176.refs_1_, bf16[3456,512]{1,0:T(8,128)(2,1)S(1)} %get-tuple-element.177.refs_2_, bf16[3456,512]{1,0:T(8,128)(2,1)S(1)} %get-tuple-element.178.refs_3_, ...), custom_call_target="tpu_custom_call" | custom-call | flops 34500000 | tf_op jit(solution)/shard_map/conv_weight_grad/pallas_call | solution.py:54
  169.9 7.3 %spread.7.refs_11_.refs_2_ = f32[128,1024]{1,0:T(8,128)S(1)} custom-call(s32[2]{0:T(128)S(1)} %pad_add_fusion.refs_0_, s32[27,2048]{1,0:T(8,128)S(1)} %bitcast.48, bf16[3456,512]{1,0:T(8,128)(2,1)S(1)} %bitcast.38, bf16[512,512]{1,0:T(8,128)(2,1)S(1)} %collective-permute-done.19.refs_6_.refs_3_, ...), custom_call_target="tpu_custom_call" | custom-call | flops 34500000 | tf_op jit(solution)/shard_map/spread/pallas_call | solution.py:54
  177.2 2.0 collective-permute-done.24.refs_10_
  179.2 3.4 %conv_weight_grad.4 = (bf16[4,64,1792]{2,1,0:T(8,128)(2,1)S(1)}, bf16[4,64,1792]{2,1,0:T(8,128)(2,1)S(1)}) custom-call(s32[2]{0:T(128)S(1)} %pad_add_fusion.refs_0_, bf16[3456,512]{1,0:T(8,128)(2,1)S(1)} %get-tuple-element.176.refs_1_, bf16[3456,512]{1,0:T(8,128)(2,1)S(1)} %get-tuple-element.177.refs_2_, bf16[3456,512]{1,0:T(8,128)(2,1)S(1)} %get-tuple-element.178.refs_3_, ...), custom_call_target="tpu_custom_call" | custom-call | flops 34500000 | tf_op jit(solution)/shard_map/conv_weight_grad/pallas_call | solution.py:54
  183.3 1.7 collective-permute-start.27
  185.3 3.3 %conv_weight_grad.5 = (bf16[4,64,1152]{2,1,0:T(8,128)(2,1)S(1)}, bf16[4,64,1152]{2,1,0:T(8,128)(2,1)S(1)}) custom-call(s32[2]{0:T(128)S(1)} %pad_add_fusion.refs_0_, bf16[3456,512]{1,0:T(8,128)(2,1)S(1)} %get-tuple-element.176.refs_1_, bf16[3456,512]{1,0:T(8,128)(2,1)S(1)} %get-tuple-element.177.refs_2_, bf16[3456,512]{1,0:T(8,128)(2,1)S(1)} %get-tuple-element.178.refs_3_, ...), custom_call_target="tpu_custom_call" | custom-call | flops 34500000 | tf_op jit(solution)/shard_map/conv_weight_grad/pallas_call | solution.py:54
  188.6 1.3 collective-permute-start.35
  190.0 4.2 %spread.8.refs_2_.refs_4_.refs_3_ = f32[128,768]{1,0:T(8,128)S(1)} custom-call(s32[2]{0:T(128)S(1)} %pad_add_fusion.refs_0_, s32[27,2048]{1,0:T(8,128)S(1)} %bitcast.49, bf16[3456,512]{1,0:T(8,128)(2,1)S(1)} %bitcast.39, bf16[512,512]{1,0:T(8,128)(2,1)S(1)} %collective-permute-done.20.refs_9_.refs_7_.refs_3_, ...), custom_call_target="tpu_custom_call" | custom-call | flops 1448999936 | tf_op jit(solution)/shard_map/spread/pallas_call | solution.py:54
  194.3 2.8 %collective-permute-start.30 = (bf16[1,64,1152]{2,1,0:T(8,128)(2,1)S(1)}, bf16[1,64,1152]{2,1,0:T(8,128)(2,1)S(1)}, u32[]{:S(2)}, u32[]{:S(2)}) collective-permute-start(bf16[1,64,1152]{2,1,0:T(8,128)(2,1)S(1)} %get-tuple-element.203.refs_6_), channel_id=1, source_target_pairs={{0,16},{4,20},{8,24},{12,28},{16,0},{20,4},{24,8},{28,12},{1,17},{... | collective-permute-start | bytes 442376 | tf_op jit(solution)/shard_map/ppermute | solution.py:1109
  197.6 4.4 %spread.9.refs_4_ = f32[128,768]{1,0:T(8,128)S(1)} custom-call(s32[2]{0:T(128)S(1)} %pad_add_fusion.refs_0_, s32[27,2048]{1,0:T(8,128)S(1)} %bitcast.50, bf16[3456,512]{1,0:T(8,128)(2,1)S(1)} %bitcast.40, bf16[512,512]{1,0:T(8,128)(2,1)S(1)} %collective-permute-done.20.refs_9_.refs_7_.refs_3_, f32[128,768]{1,0:T(8,128)S(1)} %spread.8.refs_2_.refs_4_.refs_3_, ...), custom_call_target="tpu_custom_call" | custom-call | flops 1448999936 | tf_op jit(solution)/shard_map/spread/pallas_call | solution.py:54
  202.1 4.2 %spread.10.refs_2_.refs_4_.refs_5_ = f32[128,768]{1,0:T(8,128)S(1)} custom-call(s32[2]{0:T(128)S(1)} %pad_add_fusion.refs_0_, s32[27,2048]{1,0:T(8,128)S(1)} %bitcast.51, bf16[3456,512]{1,0:T(8,128)(2,1)S(1)} %bitcast.41, bf16[512,512]{1,0:T(8,128)(2,1)S(1)} %collective-permute-done.21.refs_8_.refs_3_, f32[128,768]{1,0:T(8,128)S(1)} %spread.9.refs_4_), custom_call_target="tpu_custom_call" | custom-call | flops 1448999936 | tf_op jit(solution)/shard_map/spread/pallas_call | solution.py:54
  206.5 1.4 collective-permute-start.38
  207.9 5.3 %collective-permute-start.36 = (bf16[512,512]{1,0:T(8,128)(2,1)S(1)}, bf16[512,512]{1,0:T(8,128)(2,1)S(1)}, u32[]{:S(2)}, u32[]{:S(2)}) collective-permute-start(bf16[512,512]{1,0:T(8,128)(2,1)S(1)} %collective-permute-done.35.refs_7_), channel_id=1, source_target_pairs={{0,1},{1,0},{2,3},{3,2},{4,5},{5,4},{6,7},{7,6},{8,9},{9,8},{10,11... | collective-permute-start | bytes 1572872 | tf_op jit(solution)/shard_map/ppermute | solution.py:1109
  213.2 4.2 %spread.11.refs_2_.refs_6_ = f32[128,768]{1,0:T(8,128)S(1)} custom-call(s32[2]{0:T(128)S(1)} %pad_add_fusion.refs_0_, s32[27,2048]{1,0:T(8,128)S(1)} %bitcast.52, bf16[3456,512]{1,0:T(8,128)(2,1)S(1)} %bitcast.42, bf16[512,512]{1,0:T(8,128)(2,1)S(1)} %collective-permute-done.21.refs_8_.refs_3_, f32[128,768]{1,0:T(8,128)S(1)} %spread.10.refs_2_.refs_4_.refs_5_, ...), custom_call_target="tpu_custom_call" | custom-call | flops 1448999936 | tf_op jit(solution)/shard_map/spread/pallas_call | solution.py:54
  217.6 1.2 collective-permute-start.37
  222.3 2.9 %collective-permute-start.39 = (bf16[1,64,1792]{2,1,0:T(8,128)(2,1)S(1)}, bf16[1,64,1792]{2,1,0:T(8,128)(2,1)S(1)}, u32[]{:S(2)}, u32[]{:S(2)}) collective-permute-start(bf16[1,64,1792]{2,1,0:T(8,128)(2,1)S(1)} %get-tuple-element.222.refs_2_), channel_id=1, source_target_pairs={{0,16},{4,20},{8,24},{12,28},{16,0},{20,4},{24,8},{28,12},{1,17},{... | collective-permute-start | bytes 688136 | tf_op jit(solution)/shard_map/ppermute | solution.py:1109
  225.2 2.1 collective-permute-done.37.refs_1_
  227.6 4.1 %collective-permute-start.32 = (bf16[128,256]{1,0:T(8,128)(2,1)S(1)}, bf16[128,256]{1,0:T(8,128)(2,1)S(1)}, u32[]{:S(2)}, u32[]{:S(2)}) collective-permute-start(bf16[128,256]{1,0:T(8,128)(2,1)S(1)} %get-tuple-element.211), channel_id=1, source_target_pairs={{0,4},{4,8},{8,12},{12,16},{16,20},{20,24},{24,28},{1,5},{5,9},{9,... | collective-permute-start | bytes 196616 | tf_op jit(solution)/shard_map/ppermute | solution.py:1281
  231.7 1.9 collective-permute-start.33
  234.3 10.1 %collective-permute-done.33.refs_3_ = bf16[128,256]{1,0:T(8,128)(2,1)S(1)} collective-permute-done((bf16[128,256]{1,0:T(8,128)(2,1)S(1)}, bf16[128,256]{1,0:T(8,128)(2,1)S(1)}, u32[]{:S(2)}, u32[]{:S(2)}) %collective-permute-start.33) | collective-permute-done | bytes 65568 | tf_op jit(solution)/shard_map/ppermute | solution.py:1280
  244.4 2.1 rows_out.1
  246.6 1.1 grads_out.1
  (97 shorter events, 22.0 us)
Async XLA Ops:
  1.5 11.6 %collective-permute-start.1 = (bf16[256,128]{1,0:T(8,128)(2,1)S(1)}, bf16[256,128]{1,0:T(8,128)(2,1)S(1)}, u32[]{:S(2)}, u32[]{:S(2)}) collective-permute-start(bf16[256,128]{1,0:T(8,128)(2,1)S(1)} %get-tuple-element.246), channel_id=1, source_target_pairs={{4,0},{8,4},{12,8},{16,12},{20,16},{24,20},{28,24},{5,1},{9,5},{13... | collective-permute-start | bytes 196616 | tf_op jit(solution)/shard_map/ppermute | solution.py:1159
  3.5 6.3 %collective-permute-start = (bf16[256,128]{1,0:T(8,128)(2,1)S(1)}, bf16[256,128]{1,0:T(8,128)(2,1)S(1)}, u32[]{:S(2)}, u32[]{:S(2)}) collective-permute-start(bf16[256,128]{1,0:T(8,128)(2,1)S(1)} %get-tuple-element.247), channel_id=1, source_target_pairs={{0,4},{4,8},{8,12},{12,16},{16,20},{20,24},{24,28},{1,5},{5,9},{9,... | collective-permute-start | bytes 196616 | tf_op jit(solution)/shard_map/ppermute | solution.py:1158
  9.7 3.4 %copy-start.1 = (s32[2048,27]{0,1:T(8,128)S(1)}, s32[2048,27]{0,1:T(8,128)}, u32[]{:S(2)}) copy-start(s32[2048,27]{0,1:T(8,128)} %param.23) | copy-start | bytes 663556
  9.7 3.4 %copy-start.2 = (bf16[2048,128]{1,0:T(8,128)(2,1)S(1)}, bf16[2048,128]{1,0:T(8,128)(2,1)}, u32[]{:S(2)}) copy-start(bf16[2048,128]{1,0:T(8,128)(2,1)} %refs_6_.4) | copy-start | bytes 1572868
  12.3 18.3 %collective-permute-start.8 = (bf16[784,512]{1,0:T(8,128)(2,1)S(1)}, bf16[784,512]{1,0:T(8,128)(2,1)S(1)}, u32[]{:S(2)}, u32[]{:S(2)}) collective-permute-start(bf16[784,512]{1,0:T(8,128)(2,1)S(1)} %get-tuple-element.143), channel_id=1, source_target_pairs={{0,2},{1,3},{2,0},{3,1},{4,6},{5,7},{6,4},{7,5},{8,10},{9,11},{10,... | collective-permute-start | bytes 2408456 | tf_op jit(solution)/shard_map/ppermute | solution.py:1109
  20.6 9.4 %collective-permute-start.4 = (bf16[256,512]{1,0:T(8,128)(2,1)S(1)}, bf16[256,512]{1,0:T(8,128)(2,1)S(1)}, u32[]{:S(2)}, u32[]{:S(2)}) collective-permute-start(bf16[256,512]{1,0:T(8,128)(2,1)S(1)} %get-tuple-element.133.refs_6_), channel_id=1, source_target_pairs={{0,1},{1,0},{2,3},{3,2},{4,5},{5,4},{6,7},{7,6},{8,9},{9,8},{10,11... | collective-permute-start | bytes 786440 | tf_op jit(solution)/shard_map/ppermute | solution.py:1109
  22.5 10.2 %collective-permute-start.5 = (bf16[256,512]{1,0:T(8,128)(2,1)S(1)}, bf16[256,512]{1,0:T(8,128)(2,1)S(1)}, u32[]{:S(2)}, u32[]{:S(2)}) collective-permute-start(bf16[256,512]{1,0:T(8,128)(2,1)S(1)} %get-tuple-element.140), channel_id=1, source_target_pairs={{0,1},{1,0},{2,3},{3,2},{4,5},{5,4},{6,7},{7,6},{8,9},{9,8},{10,11... | collective-permute-start | bytes 786440 | tf_op jit(solution)/shard_map/ppermute | solution.py:1109
  30.6 19.7 %collective-permute-start.9 = (bf16[784,512]{1,0:T(8,128)(2,1)S(1)}, bf16[784,512]{1,0:T(8,128)(2,1)S(1)}, u32[]{:S(2)}, u32[]{:S(2)}) collective-permute-start(bf16[784,512]{1,0:T(8,128)(2,1)S(1)} %collective-permute-done.8.refs_10_.refs_2_.refs_3_.refs_11_), channel_id=1, source_target_pairs={{0,1},{1,0},{2,3},{3,2},{4,5},{5,4},{6,7},{7,6},{8,9},{9,8},{10,11... | collective-permute-start | bytes 2408456 | tf_op jit(solution)/shard_map/ppermute | solution.py:1109
  32.8 17.5 %collective-permute-start.6 = (bf16[512,512]{1,0:T(8,128)(2,1)S(1)}, bf16[512,512]{1,0:T(8,128)(2,1)S(1)}, u32[]{:S(2)}, u32[]{:S(2)}) collective-permute-start(bf16[512,512]{1,0:T(8,128)(2,1)S(1)} %pad_maximum_fusion), channel_id=1, source_target_pairs={{0,2},{1,3},{2,0},{3,1},{4,6},{5,7},{6,4},{7,5},{8,10},{9,11},{10,... | collective-permute-start | bytes 1572872 | tf_op jit(solution)/shard_map/ppermute | solution.py:1109
  40.8 1.6 collective-permute-start.3
  41.2 9.1 %collective-permute-start.7 = (bf16[272,512]{1,0:T(8,128)(2,1)S(1)}, bf16[272,512]{1,0:T(8,128)(2,1)S(1)}, u32[]{:S(2)}, u32[]{:S(2)}) collective-permute-start(bf16[272,512]{1,0:T(8,128)(2,1)S(1)} %get-tuple-element.142), channel_id=1, source_target_pairs={{0,1},{1,0},{2,3},{3,2},{4,5},{5,4},{6,7},{7,6},{8,9},{9,8},{10,11... | collective-permute-start | bytes 835592 | tf_op jit(solution)/shard_map/ppermute | solution.py:1109
  41.4 8.9 %collective-permute-start.2 = (bf16[256,512]{1,0:T(8,128)(2,1)S(1)}, bf16[256,512]{1,0:T(8,128)(2,1)S(1)}, u32[]{:S(2)}, u32[]{:S(2)}) collective-permute-start(bf16[256,512]{1,0:T(8,128)(2,1)S(1)} %get-tuple-element.135.refs_6_), channel_id=1, source_target_pairs={{0,1},{1,0},{2,3},{3,2},{4,5},{5,4},{6,7},{7,6},{8,9},{9,8},{10,11... | collective-permute-start | bytes 786440 | tf_op jit(solution)/shard_map/ppermute | solution.py:1109
  41.7 8.7 %copy-start.3 = (bf16[128,512]{1,0:T(8,128)(2,1)S(1)}, bf16[128,512]{1,0:T(8,128)(2,1)}, u32[]{:S(2)}) copy-start(bf16[128,512]{1,0:T(8,128)(2,1)} %refs_9_.3) | copy-start | bytes 393220
  42.4 42.7 %collective-permute-start.13 = (bf16[1408,512]{1,0:T(8,128)(2,1)S(1)}, bf16[1408,512]{1,0:T(8,128)(2,1)S(1)}, u32[]{:S(2)}, u32[]{:S(2)}) collective-permute-start(bf16[1408,512]{1,0:T(8,128)(2,1)S(1)} %get-tuple-element.154), channel_id=1, source_target_pairs={{0,2},{1,3},{2,0},{3,1},{4,6},{5,7},{6,4},{7,5},{8,10},{9,11},{10,... | collective-permute-start | bytes 4325384 | tf_op jit(solution)/shard_map/ppermute | solution.py:1109
  52.1 2.2 collective-permute-start.10
  52.7 33.0 %collective-permute-start.12 = (bf16[1536,512]{1,0:T(8,128)(2,1)S(1)}, bf16[1536,512]{1,0:T(8,128)(2,1)S(1)}, u32[]{:S(2)}, u32[]{:S(2)}) collective-permute-start(bf16[1536,512]{1,0:T(8,128)(2,1)S(1)} %get-tuple-element.152), channel_id=1, source_target_pairs={{0,1},{1,0},{2,3},{3,2},{4,5},{5,4},{6,7},{7,6},{8,9},{9,8},{10,11... | collective-permute-start | bytes 4718600 | tf_op jit(solution)/shard_map/ppermute | solution.py:1109
  54.3 34.6 %copy-start.5 = (bf16[512,512]{1,0:T(8,128)(2,1)S(1)}, bf16[512,512]{1,0:T(8,128)(2,1)}, u32[]{:S(2)}) copy-start(bf16[512,512]{1,0:T(8,128)(2,1)} %refs_5_.1) | copy-start | bytes 1572868
  54.3 34.6 %copy-start.6 = (bf16[512,512]{1,0:T(8,128)(2,1)S(1)}, bf16[512,512]{1,0:T(8,128)(2,1)}, u32[]{:S(2)}) copy-start(bf16[512,512]{1,0:T(8,128)(2,1)} %refs_6_.5) | copy-start | bytes 1572868
  54.3 34.6 %copy-start.7 = (bf16[2048,128]{1,0:T(8,128)(2,1)S(1)}, bf16[2048,128]{1,0:T(8,128)(2,1)}, u32[]{:S(2)}) copy-start(bf16[2048,128]{1,0:T(8,128)(2,1)} %refs_4_.1) | copy-start | bytes 1572868
  54.3 34.6 %copy-start.8 = (bf16[128,512]{1,0:T(8,128)(2,1)S(1)}, bf16[128,512]{1,0:T(8,128)(2,1)}, u32[]{:S(2)}) copy-start(bf16[128,512]{1,0:T(8,128)(2,1)} %refs_7_.3) | copy-start | bytes 393220
  85.2 3.7 %collective-permute-start.14 = (bf16[1408,512]{1,0:T(8,128)(2,1)S(1)}, bf16[1408,512]{1,0:T(8,128)(2,1)S(1)}, u32[]{:S(2)}, u32[]{:S(2)}) collective-permute-start(bf16[1408,512]{1,0:T(8,128)(2,1)S(1)} %collective-permute-done.13.refs_13_), channel_id=1, source_target_pairs={{0,1},{1,0},{2,3},{3,2},{4,5},{5,4},{6,7},{7,6},{8,9},{9,8},{10,11... | collective-permute-start | bytes 4325384 | tf_op jit(solution)/shard_map/ppermute | solution.py:1109
  85.6 3.2 %collective-permute-start.11 = (bf16[256,512]{1,0:T(8,128)(2,1)S(1)}, bf16[256,512]{1,0:T(8,128)(2,1)S(1)}, u32[]{:S(2)}, u32[]{:S(2)}) collective-permute-start(bf16[256,512]{1,0:T(8,128)(2,1)S(1)} %get-tuple-element.150), channel_id=1, source_target_pairs={{0,1},{1,0},{2,3},{3,2},{4,5},{5,4},{6,7},{7,6},{8,9},{9,8},{10,11... | collective-permute-start | bytes 786440 | tf_op jit(solution)/shard_map/ppermute | solution.py:1109
  98.0 2.5 %collective-permute-start.15 = (bf16[256,512]{1,0:T(8,128)(2,1)S(1)}, bf16[256,512]{1,0:T(8,128)(2,1)S(1)}, u32[]{:S(2)}, u32[]{:S(2)}) collective-permute-start(bf16[256,512]{1,0:T(8,128)(2,1)S(1)} %get-tuple-element.157), channel_id=1, source_target_pairs={{0,1},{1,0},{2,3},{3,2},{4,5},{5,4},{6,7},{7,6},{8,9},{9,8},{10,11... | collective-permute-start | bytes 786440 | tf_op jit(solution)/shard_map/ppermute | solution.py:1109
  100.5 19.4 %collective-permute-start.16 = (bf16[2,8,64,1152]{3,2,1,0:T(8,128)(2,1)S(1)}, bf16[2,8,64,1152]{3,2,1,0:T(8,128)(2,1)S(1)}, u32[]{:S(2)}, u32[]{:S(2)}) collective-permute-start(bf16[2,8,64,1152]{3,2,1,0:T(8,128)(2,1)S(1)} %second_send.1.refs_6_), channel_id=1, source_target_pairs={{0,1},{1,0},{2,3},{3,2},{4,5},{5,4},{6,7},{7,6},{8,9},{9,8},{10,11... | collective-permute-start | bytes 7077896 | tf_op jit(solution)/shard_map/ppermute | solution.py:1109
  122.0 27.2 %collective-permute-start.18 = (bf16[8,64,1152]{2,1,0:T(8,128)(2,1)S(1)}, bf16[8,64,1152]{2,1,0:T(8,128)(2,1)S(1)}, u32[]{:S(2)}, u32[]{:S(2)}) collective-permute-start(bf16[8,64,1152]{2,1,0:T(8,128)(2,1)S(1)} %get-tuple-element.175), channel_id=1, source_target_pairs={{0,2},{1,3},{2,0},{3,1},{4,6},{5,7},{6,4},{7,5},{8,10},{9,11},{10,... | collective-permute-start | bytes 3538952 | tf_op jit(solution)/shard_map/ppermute | solution.py:1109
  143.5 2.3 collective-permute-start.17
  148.2 13.2 %collective-permute-start.20 = (bf16[512,512]{1,0:T(8,128)(2,1)S(1)}, bf16[512,512]{1,0:T(8,128)(2,1)S(1)}, u32[]{:S(2)}, u32[]{:S(2)}) collective-permute-start(bf16[512,512]{1,0:T(8,128)(2,1)S(1)} %get-tuple-element.174.refs_3_.refs_5_), channel_id=1, source_target_pairs={{0,2},{1,3},{2,0},{3,1},{4,6},{5,7},{6,4},{7,5},{8,10},{9,11},{10,... | collective-permute-start | bytes 1572872 | tf_op jit(solution)/shard_map/ppermute | solution.py:1109
  149.6 13.7 %collective-permute-start.23 = (bf16[4,64,1152]{2,1,0:T(8,128)(2,1)S(1)}, bf16[4,64,1152]{2,1,0:T(8,128)(2,1)S(1)}, u32[]{:S(2)}, u32[]{:S(2)}) collective-permute-start(bf16[4,64,1152]{2,1,0:T(8,128)(2,1)S(1)} %get-tuple-element.189), channel_id=1, source_target_pairs={{0,4},{4,0},{8,12},{12,8},{16,20},{20,16},{24,28},{28,24},{1,5},{5... | collective-permute-start | bytes 1769480 | tf_op jit(solution)/shard_map/ppermute | solution.py:1109
  158.3 4.4 %collective-permute-start.22 = (bf16[2,8,80,128]{3,2,1,0:T(8,128)(2,1)S(1)}, bf16[2,8,80,128]{3,2,1,0:T(8,128)(2,1)S(1)}, u32[]{:S(2)}, u32[]{:S(2)}) collective-permute-start(bf16[2,8,80,128]{3,2,1,0:T(8,128)(2,1)S(1)} %get-tuple-element.185), channel_id=1, source_target_pairs={{0,1},{1,0},{2,3},{3,2},{4,5},{5,4},{6,7},{7,6},{8,9},{9,8},{10,11... | collective-permute-start | bytes 983048 | tf_op jit(solution)/shard_map/ppermute | solution.py:1109
  159.6 6.4 %collective-permute-start.19 = (bf16[512,512]{1,0:T(8,128)(2,1)S(1)}, bf16[512,512]{1,0:T(8,128)(2,1)S(1)}, u32[]{:S(2)}, u32[]{:S(2)}) collective-permute-start(bf16[512,512]{1,0:T(8,128)(2,1)S(1)} %get-tuple-element.174.refs_3_.refs_5_), channel_id=1, source_target_pairs={{0,1},{1,0},{2,3},{3,2},{4,5},{5,4},{6,7},{7,6},{8,9},{9,8},{10,11... | collective-permute-start | bytes 1572872 | tf_op jit(solution)/shard_map/ppermute | solution.py:1109
  161.4 4.5 %collective-permute-start.21 = (bf16[512,512]{1,0:T(8,128)(2,1)S(1)}, bf16[512,512]{1,0:T(8,128)(2,1)S(1)}, u32[]{:S(2)}, u32[]{:S(2)}) collective-permute-start(bf16[512,512]{1,0:T(8,128)(2,1)S(1)} %collective-permute-done.20.refs_9_.refs_7_.refs_3_), channel_id=1, source_target_pairs={{0,1},{1,0},{2,3},{3,2},{4,5},{5,4},{6,7},{7,6},{8,9},{9,8},{10,11... | collective-permute-start | bytes 1572872 | tf_op jit(solution)/shard_map/ppermute | solution.py:1109
  165.1 14.2 %collective-permute-start.24 = (bf16[8,64,640]{2,1,0:T(8,128)(2,1)S(1)}, bf16[8,64,640]{2,1,0:T(8,128)(2,1)S(1)}, u32[]{:S(2)}, u32[]{:S(2)}) collective-permute-start(bf16[8,64,640]{2,1,0:T(8,128)(2,1)S(1)} %get-tuple-element.195), channel_id=1, source_target_pairs={{0,2},{1,3},{2,0},{3,1},{4,6},{5,7},{6,4},{7,5},{8,10},{9,11},{10,... | collective-permute-start | bytes 1966088 | tf_op jit(solution)/shard_map/ppermute | solution.py:1109
  169.2 15.8 %collective-permute-start.25 = (bf16[4,64,1152]{2,1,0:T(8,128)(2,1)S(1)}, bf16[4,64,1152]{2,1,0:T(8,128)(2,1)S(1)}, u32[]{:S(2)}, u32[]{:S(2)}) collective-permute-start(bf16[4,64,1152]{2,1,0:T(8,128)(2,1)S(1)} %get-tuple-element.197), channel_id=1, source_target_pairs={{0,4},{4,0},{8,12},{12,8},{16,20},{20,16},{24,28},{28,24},{1,5},{5... | collective-permute-start | bytes 1769480 | tf_op jit(solution)/shard_map/ppermute | solution.py:1109
  182.7 23.6 %collective-permute-start.28 = (bf16[4,64,1792]{2,1,0:T(8,128)(2,1)S(1)}, bf16[4,64,1792]{2,1,0:T(8,128)(2,1)S(1)}, u32[]{:S(2)}, u32[]{:S(2)}) collective-permute-start(bf16[4,64,1792]{2,1,0:T(8,128)(2,1)S(1)} %get-tuple-element.204), channel_id=1, source_target_pairs={{0,4},{4,0},{8,12},{12,8},{16,20},{20,16},{24,28},{28,24},{1,5},{5... | collective-permute-start | bytes 2752520 | tf_op jit(solution)/shard_map/ppermute | solution.py:1109
  183.3 10.9 %collective-permute-start.27 = (bf16[2,64,1152]{2,1,0:T(8,128)(2,1)S(1)}, bf16[2,64,1152]{2,1,0:T(8,128)(2,1)S(1)}, u32[]{:S(2)}, u32[]{:S(2)}) collective-permute-start(bf16[2,64,1152]{2,1,0:T(8,128)(2,1)S(1)} %get-tuple-element.193.refs_5_), channel_id=1, source_target_pairs={{0,8},{4,12},{8,0},{12,4},{16,24},{20,28},{24,16},{28,20},{1,9},{5... | collective-permute-start | bytes 884744 | tf_op jit(solution)/shard_map/ppermute | solution.py:1109
  185.2 11.9 %collective-permute-start.26 = (bf16[2,64,1152]{2,1,0:T(8,128)(2,1)S(1)}, bf16[2,64,1152]{2,1,0:T(8,128)(2,1)S(1)}, u32[]{:S(2)}, u32[]{:S(2)}) collective-permute-start(bf16[2,64,1152]{2,1,0:T(8,128)(2,1)S(1)} %get-tuple-element.198.refs_10_), channel_id=1, source_target_pairs={{0,8},{4,12},{8,0},{12,4},{16,24},{20,28},{24,16},{28,20},{1,9},{5... | collective-permute-start | bytes 884744 | tf_op jit(solution)/shard_map/ppermute | solution.py:1109
  188.6 19.4 %collective-permute-start.35 = (bf16[512,512]{1,0:T(8,128)(2,1)S(1)}, bf16[512,512]{1,0:T(8,128)(2,1)S(1)}, u32[]{:S(2)}, u32[]{:S(2)}) collective-permute-start(bf16[512,512]{1,0:T(8,128)(2,1)S(1)} %get-tuple-element.218), channel_id=1, source_target_pairs={{0,2},{1,3},{2,0},{3,1},{4,6},{5,7},{6,4},{7,5},{8,10},{9,11},{10,... | collective-permute-start | bytes 1572872 | tf_op jit(solution)/shard_map/ppermute | solution.py:1109
  189.8 27.6 %collective-permute-start.31 = (bf16[4,64,1152]{2,1,0:T(8,128)(2,1)S(1)}, bf16[4,64,1152]{2,1,0:T(8,128)(2,1)S(1)}, u32[]{:S(2)}, u32[]{:S(2)}) collective-permute-start(bf16[4,64,1152]{2,1,0:T(8,128)(2,1)S(1)} %get-tuple-element.206), channel_id=1, source_target_pairs={{0,4},{4,0},{8,12},{12,8},{16,20},{20,16},{24,28},{28,24},{1,5},{5... | collective-permute-start | bytes 1769480 | tf_op jit(solution)/shard_map/ppermute | solution.py:1109
  194.3 18.9 %collective-permute-start.30 = (bf16[1,64,1152]{2,1,0:T(8,128)(2,1)S(1)}, bf16[1,64,1152]{2,1,0:T(8,128)(2,1)S(1)}, u32[]{:S(2)}, u32[]{:S(2)}) collective-permute-start(bf16[1,64,1152]{2,1,0:T(8,128)(2,1)S(1)} %get-tuple-element.203.refs_6_), channel_id=1, source_target_pairs={{0,16},{4,20},{8,24},{12,28},{16,0},{20,4},{24,8},{28,12},{1,17},{... | collective-permute-start | bytes 442376 | tf_op jit(solution)/shard_map/ppermute | solution.py:1109
  197.2 16.0 %collective-permute-start.29 = (bf16[1,64,1152]{2,1,0:T(8,128)(2,1)S(1)}, bf16[1,64,1152]{2,1,0:T(8,128)(2,1)S(1)}, u32[]{:S(2)}, u32[]{:S(2)}) collective-permute-start(bf16[1,64,1152]{2,1,0:T(8,128)(2,1)S(1)} %get-tuple-element.201.refs_5_), channel_id=1, source_target_pairs={{0,16},{4,20},{8,24},{12,28},{16,0},{20,4},{24,8},{28,12},{1,17},{... | collective-permute-start | bytes 442376 | tf_op jit(solution)/shard_map/ppermute | solution.py:1109
  206.5 15.6 %collective-permute-start.38 = (bf16[2,64,1792]{2,1,0:T(8,128)(2,1)S(1)}, bf16[2,64,1792]{2,1,0:T(8,128)(2,1)S(1)}, u32[]{:S(2)}, u32[]{:S(2)}) collective-permute-start(bf16[2,64,1792]{2,1,0:T(8,128)(2,1)S(1)} %get-tuple-element.205.refs_5_), channel_id=1, source_target_pairs={{0,8},{4,12},{8,0},{12,4},{16,24},{20,28},{24,16},{28,20},{1,9},{5... | collective-permute-start | bytes 1376264 | tf_op jit(solution)/shard_map/ppermute | solution.py:1109
  207.9 36.5 %collective-permute-start.36 = (bf16[512,512]{1,0:T(8,128)(2,1)S(1)}, bf16[512,512]{1,0:T(8,128)(2,1)S(1)}, u32[]{:S(2)}, u32[]{:S(2)}) collective-permute-start(bf16[512,512]{1,0:T(8,128)(2,1)S(1)} %collective-permute-done.35.refs_7_), channel_id=1, source_target_pairs={{0,1},{1,0},{2,3},{3,2},{4,5},{5,4},{6,7},{7,6},{8,9},{9,8},{10,11... | collective-permute-start | bytes 1572872 | tf_op jit(solution)/shard_map/ppermute | solution.py:1109
  217.6 9.8 %collective-permute-start.37 = (bf16[2,64,1152]{2,1,0:T(8,128)(2,1)S(1)}, bf16[2,64,1152]{2,1,0:T(8,128)(2,1)S(1)}, u32[]{:S(2)}, u32[]{:S(2)}) collective-permute-start(bf16[2,64,1152]{2,1,0:T(8,128)(2,1)S(1)} %get-tuple-element.207.refs_7_), channel_id=1, source_target_pairs={{0,8},{4,12},{8,0},{12,4},{16,24},{20,28},{24,16},{28,20},{1,9},{5... | collective-permute-start | bytes 884744 | tf_op jit(solution)/shard_map/ppermute | solution.py:1109
  218.8 12.9 %collective-permute-start.34 = (bf16[512,256]{1,0:T(8,128)(2,1)S(1)}, bf16[512,256]{1,0:T(8,128)(2,1)S(1)}, u32[]{:S(2)}, u32[]{:S(2)}) collective-permute-start(bf16[512,256]{1,0:T(8,128)(2,1)S(1)} %get-tuple-element.216), channel_id=1, source_target_pairs={{0,1},{1,0},{2,3},{3,2},{4,5},{5,4},{6,7},{7,6},{8,9},{9,8},{10,11... | collective-permute-start | bytes 786440 | tf_op jit(solution)/shard_map/ppermute | solution.py:1109
  222.3 24.3 %collective-permute-start.39 = (bf16[1,64,1792]{2,1,0:T(8,128)(2,1)S(1)}, bf16[1,64,1792]{2,1,0:T(8,128)(2,1)S(1)}, u32[]{:S(2)}, u32[]{:S(2)}) collective-permute-start(bf16[1,64,1792]{2,1,0:T(8,128)(2,1)S(1)} %get-tuple-element.222.refs_2_), channel_id=1, source_target_pairs={{0,16},{4,20},{8,24},{12,28},{16,0},{20,4},{24,8},{28,12},{1,17},{... | collective-permute-start | bytes 688136 | tf_op jit(solution)/shard_map/ppermute | solution.py:1109
  227.5 19.1 %collective-permute-start.40 = (bf16[1,64,1152]{2,1,0:T(8,128)(2,1)S(1)}, bf16[1,64,1152]{2,1,0:T(8,128)(2,1)S(1)}, u32[]{:S(2)}, u32[]{:S(2)}) collective-permute-start(bf16[1,64,1152]{2,1,0:T(8,128)(2,1)S(1)} %get-tuple-element.223.refs_9_), channel_id=1, source_target_pairs={{0,16},{4,20},{8,24},{12,28},{16,0},{20,4},{24,8},{28,12},{1,17},{... | collective-permute-start | bytes 442376 | tf_op jit(solution)/shard_map/ppermute | solution.py:1109
  227.6 6.8 %collective-permute-start.32 = (bf16[128,256]{1,0:T(8,128)(2,1)S(1)}, bf16[128,256]{1,0:T(8,128)(2,1)S(1)}, u32[]{:S(2)}, u32[]{:S(2)}) collective-permute-start(bf16[128,256]{1,0:T(8,128)(2,1)S(1)} %get-tuple-element.211), channel_id=1, source_target_pairs={{0,4},{4,8},{8,12},{12,16},{16,20},{20,24},{24,28},{1,5},{5,9},{9,... | collective-permute-start | bytes 196616 | tf_op jit(solution)/shard_map/ppermute | solution.py:1281
  231.7 12.7 %collective-permute-start.33 = (bf16[128,256]{1,0:T(8,128)(2,1)S(1)}, bf16[128,256]{1,0:T(8,128)(2,1)S(1)}, u32[]{:S(2)}, u32[]{:S(2)}) collective-permute-start(bf16[128,256]{1,0:T(8,128)(2,1)S(1)} %get-tuple-element.212), channel_id=1, source_target_pairs={{4,0},{8,4},{12,8},{16,12},{20,16},{24,20},{28,24},{5,1},{9,5},{13... | collective-permute-start | bytes 196616 | tf_op jit(solution)/shard_map/ppermute | solution.py:1280
  (2 other events, 4.3 us)
where the time goes:
time: 252 us; the launch traced here: 248 us
  Pallas kernels  173 us (69%)
  starting transfers between devices  46.3 us (18%)
  waiting for transfers between devices  24.8 us (10%)
    pallas_call x40, Pallas kernels, call(): pl.pallas_call(body, out_shape=[o for o, spec in outputs], in_specs=[spec...  173 us
    ppermute x37, starting transfers between devices, swap(): lax.ppermute(values, axis, [(i, i ^ e) for i in range(lax.axis_size(axis))])  34.1 us
    ppermute x37, waiting for transfers between devices, swap(): lax.ppermute(values, axis, [(i, i ^ e) for i in range(lax.axis_size(axis))])  12.1 us
    ppermute x1, waiting for transfers between devices, shards(): from_above = lax.ppermute(to_below, 'pts', downs)  10.1 us
  transfers between devices with their start and end apart: 41, of which 13 were waited for; matrix products, arithmetic and copies ran while one was open for 0% of the time, Pallas kernels for 65%

commit v1 on v0

--- a/solution.py
+++ b/solution.py
@@ -1169,7 +1169,7 @@
         (conv_bias, cpe_bias, cpe_gain, cpe_shift, first_gain, first_shift, proj_bias, second_gain, second_shift, output_bias),
         hidden_bias,
         query_value_bias,
-        first=(low,),
+        first=(high,),
     )
     far = swap(away_pack, 2)
     near = swap(near_pack, 1)

time: 252 us -> 250 us (level)
  transfers between devices with their start and end apart: 41 -> 41, of which waited for: 13 -> 11; matrix products, arithmetic and copies ran while one was open for 0% -> 0% of each run, Pallas kernels for 65% -> 66%
where the time goes in v1:
time: 250 us; the launch traced here: 246 us
  Pallas kernels  173 us (69%)
  starting transfers between devices  45.9 us (18%)
  waiting for transfers between devices  23.1 us (9%)
    pallas_call x40, Pallas kernels, call(): pl.pallas_call(body, out_shape=[o for o, spec in outputs], in_specs=[spec...  173 us
    ppermute x37, starting transfers between devices, swap(): lax.ppermute(values, axis, [(i, i ^ e) for i in range(lax.axis_size(axis))])  33.7 us
    ppermute x37, waiting for transfers between devices, swap(): lax.ppermute(values, axis, [(i, i ^ e) for i in range(lax.axis_size(axis))])  11.8 us
    ppermute x1, waiting for transfers between devices, shards(): from_above = lax.ppermute(to_below, 'pts', downs)  10.7 us
  transfers between devices with their start and end apart: 41, of which 11 were waited for; matrix products, arithmetic and copies ran while one was open for 0% of the time, Pallas kernels for 66%

profile of v1, /device:TPU:5, one launch (start us, length us, event | category | flops | bytes accessed | tf_op | source)
XLA Modules:
  0.0 245.8 jit_solution(7084953805223491664)
XLA Ops:
  1.5 1.9 collective-permute-start.1
  3.5 4.3 %collective-permute-start = (bf16[256,128]{1,0:T(8,128)(2,1)S(1)}, bf16[256,128]{1,0:T(8,128)(2,1)S(1)}, u32[]{:S(2)}, u32[]{:S(2)}) collective-permute-start(bf16[256,128]{1,0:T(8,128)(2,1)S(1)} %get-tuple-element.247), channel_id=1, source_target_pairs={{0,4},{4,8},{8,12},{12,16},{16,20},{20,24},{24,28},{1,5},{5,9},{9,... | collective-permute-start | bytes 196616 | tf_op jit(solution)/shard_map/ppermute | solution.py:1158
  7.8 2.6 %prepare.1 = (bf16[784,512]{1,0:T(8,128)(2,1)S(1)}, bf16[272,512]{1,0:T(8,128)(2,1)S(1)}, bf16[384,512]{1,0:T(8,128)(2,1)S(1)}, f32[16,128]{1,0:T(8,128)S(1)}, s32[1,1024]{1,0:T(1,128)S(1)}) custom-call(s32[2]{0:T(128)S(1)} %pad_add_fusion.refs_0_, bf16[3,512,128]{2,1,0:T(8,128)(2,1)} %bitcast.54, bf16[128,512]{1,0:T(8,128)(2,1)} %refs_9_.3, ...), custom_call_target="tpu_custom_call" | custom-call | flops 3449999872 | tf_op jit(solution)/shard_map/prepare/pallas_call | solution.py:54
  10.4 1.3 collective-permute-start.8
  11.7 7.4 %conv_forward.4 = (bf16[256,512]{1,0:T(8,128)(2,1)S(1)}, bf16[256,512]{1,0:T(8,128)(2,1)S(1)}, bf16[3456,512]{1,0:T(8,128)(2,1)S(1)}, bf16[1408,512]{1,0:T(8,128)(2,1)S(1)}, bf16[1536,512]{1,0:T(8,128)(2,1)S(1)}) custom-call(s32[2]{0:T(128)S(1)} %pad_add_fusion.refs_0_, bf16[256,128]{1,0:T(8,128)(2,1)S(1)} %collective-permute-done.refs_1_, ...), custom_call_target="tpu_custom_call" | custom-call | flops 2587500032 | tf_op jit(solution)/shard_map/conv_forward/pallas_call | solution.py:54
  19.1 1.8 collective-permute-start.4
  21.0 7.4 %conv_forward.5 = (bf16[256,512]{1,0:T(8,128)(2,1)S(1)}, bf16[256,512]{1,0:T(8,128)(2,1)S(1)}, bf16[3456,512]{1,0:T(8,128)(2,1)S(1)}) custom-call(s32[2]{0:T(128)S(1)} %pad_add_fusion.refs_0_, bf16[256,128]{1,0:T(8,128)(2,1)S(1)} %collective-permute-done.refs_1_, bf16[2048,128]{1,0:T(8,128)(2,1)S(1)} %copy-done.2, ...), custom_call_target="tpu_custom_call" | custom-call | flops 2587500032 | tf_op jit(solution)/shard_map/conv_forward/pallas_call | solution.py:54
  28.6 2.3 collective-permute-start.9
  30.9 1.3 collective-permute-start.6
  32.2 7.2 %conv_forward.6 = (bf16[256,512]{1,0:T(8,128)(2,1)S(1)}, bf16[256,512]{1,0:T(8,128)(2,1)S(1)}, bf16[3456,512]{1,0:T(8,128)(2,1)S(1)}) custom-call(s32[2]{0:T(128)S(1)} %pad_add_fusion.refs_0_, bf16[256,128]{1,0:T(8,128)(2,1)S(1)} %collective-permute-done.refs_1_, bf16[2048,128]{1,0:T(8,128)(2,1)S(1)} %copy-done.2, ...), custom_call_target="tpu_custom_call" | custom-call | flops 2587500032 | tf_op jit(solution)/shard_map/conv_forward/pallas_call | solution.py:54
  41.2 7.2 %conv_forward.7 = (f32[256,512]{1,0:T(8,128)S(1)}, f32[256,512]{1,0:T(8,128)S(1)}, bf16[3456,512]{1,0:T(8,128)(2,1)S(1)}) custom-call(s32[2]{0:T(128)S(1)} %pad_add_fusion.refs_0_, bf16[256,128]{1,0:T(8,128)(2,1)S(1)} %collective-permute-done.refs_1_, bf16[2048,128]{1,0:T(8,128)(2,1)S(1)} %copy-done.2, ...), custom_call_target="tpu_custom_call" | custom-call | flops 172500000 | tf_op jit(solution)/shard_map/conv_forward/pallas_call | solution.py:54
  48.5 1.7 first_rows.1
  50.9 1.2 triple_half.1.refs_0_
  52.4 30.9 %attend_forward.1 = (bf16[3,256,1024]{2,1,0:T(8,128)(2,1)S(1)}, f32[256,1024]{1,0:T(8,128)S(1)}, bf16[256,512]{1,0:T(8,128)(2,1)S(1)}, bf16[256,512]{1,0:T(8,128)(2,1)S(1)}, f32[16,1024]{1,0:T(8,128)S(1)}) custom-call(bf16[3,256,512]{2,1,0:T(8,128)(2,1)S(1)} %triple_half.1.refs_0_, bf16[512,512]{1,0:T(8,128)(2,1)S(1)} %collective-permute-done.10.refs_1_.refs_4_, ...), custom_call_target="tpu_custom_call" | custom-call | flops 7245000192 | tf_op jit(solution)/shard_map/attend_forward/pallas_call | solution.py:54
  83.9 3.1 %collective-permute-done.11.refs_2_.refs_6_ = bf16[256,512]{1,0:T(8,128)(2,1)S(1)} collective-permute-done((bf16[256,512]{1,0:T(8,128)(2,1)S(1)}, bf16[256,512]{1,0:T(8,128)(2,1)S(1)}, u32[]{:S(2)}, u32[]{:S(2)}) %collective-permute-start.11) | collective-permute-done | bytes 262176 | tf_op jit(solution)/shard_map/ppermute | solution.py:1109
  87.0 9.1 %second_rows.1 = (bf16[512,128]{1,0:T(8,128)(2,1)S(1)}, bf16[512,128]{1,0:T(8,128)(2,1)S(1)}, bf16[512,256]{1,0:T(8,128)(2,1)S(1)}, bf16[4,512,512]{2,1,0:T(8,12...) custom-call(s32[2]{0:T(128)S(1)} %pad_add_fusion.refs_0_, ...), custom_call_target="tpu_custom_call" | custom-call | flops 3449999872 | tf_op jit(solution)/shard_map/second_rows/pallas_call | solution.py:54
  96.6 2.1 second_send.1.refs_6_
  98.8 19.2 %attend_backward.2.refs_8_.refs_0_.refs_1_ = bf16[3,128,1024]{2,1,0:T(8,128)(2,1)S(1)} custom-call(bf16[3,256,1024]{2,1,0:T(8,128)(2,1)S(1)} %get-tuple-element.148.refs_0_, s32[1,1024]{1,0:T(1,128)S(1)} %get-tuple-element.147.refs_5_.refs_1_, bf16[256,512]{1,0:T(8,128)(2,1)S(1)} %get-tuple-element.156.refs_2_, ...), custom_call_target="tpu_custom_call" | custom-call | flops 6554999808 | tf_op jit(solution)/shard_map/attend_backward/pallas_call | solution.py:54
  118.1 2.1 second_keep.1
  120.2 1.3 collective-permute-start.18
  121.5 19.6 %attend_backward.3.refs_1_.refs_2_ = bf16[3,128,1024]{2,1,0:T(8,128)(2,1)S(1)} custom-call(bf16[3,256,1024]{2,1,0:T(8,128)(2,1)S(1)} %get-tuple-element.148.refs_0_, s32[1,1024]{1,0:T(1,128)S(1)} %get-tuple-element.147.refs_5_.refs_1_, bf16[256,512]{1,0:T(8,128)(2,1)S(1)} %get-tuple-element.156.refs_2_, ...), custom_call_target="tpu_custom_call" | custom-call | flops 6554999808 | tf_op jit(solution)/shard_map/attend_backward/pallas_call | solution.py:54
  144.4 2.4 third_rows.1
  147.8 7.3 %spread.6.refs_6_.refs_8_.refs_1_ = f32[128,1024]{1,0:T(8,128)S(1)} custom-call(s32[2]{0:T(128)S(1)} %pad_add_fusion.refs_0_, s32[27,2048]{1,0:T(8,128)S(1)} %bitcast.47, bf16[3456,512]{1,0:T(8,128)(2,1)S(1)} %bitcast.37, bf16[512,512]{1,0:T(8,128)(2,1)S(1)} %get-tuple-element.174.refs_3_.refs_5_, ...), custom_call_target="tpu_custom_call" | custom-call | flops 34500000 | tf_op jit(solution)/shard_map/spread/pallas_call | solution.py:54
  155.1 1.3 cpe_weights.1
  156.4 1.3 collective-permute-start.22
  157.8 2.2 collective-permute-done.20.refs_9_.refs_7_.refs_3_
  160.0 1.2 collective-permute-start.21
  161.4 1.8 third_weights.1
  163.2 1.3 collective-permute-start.24
  164.5 3.3 %conv_weight_grad.3 = (bf16[4,64,1152]{2,1,0:T(8,128)(2,1)S(1)}, bf16[4,64,1152]{2,1,0:T(8,128)(2,1)S(1)}) custom-call(s32[2]{0:T(128)S(1)} %pad_add_fusion.refs_0_, bf16[3456,512]{1,0:T(8,128)(2,1)S(1)} %get-tuple-element.176.refs_1_, bf16[3456,512]{1,0:T(8,128)(2,1)S(1)} %get-tuple-element.177.refs_2_, bf16[3456,512]{1,0:T(8,128)(2,1)S(1)} %get-tuple-element.178.refs_3_, ...), custom_call_target="tpu_custom_call" | custom-call | flops 34500000 | tf_op jit(solution)/shard_map/conv_weight_grad/pallas_call | solution.py:54
  168.5 7.3 %spread.7.refs_11_.refs_2_ = f32[128,1024]{1,0:T(8,128)S(1)} custom-call(s32[2]{0:T(128)S(1)} %pad_add_fusion.refs_0_, s32[27,2048]{1,0:T(8,128)S(1)} %bitcast.48, bf16[3456,512]{1,0:T(8,128)(2,1)S(1)} %bitcast.38, bf16[512,512]{1,0:T(8,128)(2,1)S(1)} %collective-permute-done.19.refs_6_.refs_3_, ...), custom_call_target="tpu_custom_call" | custom-call | flops 34500000 | tf_op jit(solution)/shard_map/spread/pallas_call | solution.py:54
  175.8 1.6 collective-permute-done.24.refs_10_
  177.3 3.4 %conv_weight_grad.4 = (bf16[4,64,1792]{2,1,0:T(8,128)(2,1)S(1)}, bf16[4,64,1792]{2,1,0:T(8,128)(2,1)S(1)}) custom-call(s32[2]{0:T(128)S(1)} %pad_add_fusion.refs_0_, bf16[3456,512]{1,0:T(8,128)(2,1)S(1)} %get-tuple-element.176.refs_1_, bf16[3456,512]{1,0:T(8,128)(2,1)S(1)} %get-tuple-element.177.refs_2_, bf16[3456,512]{1,0:T(8,128)(2,1)S(1)} %get-tuple-element.178.refs_3_, ...), custom_call_target="tpu_custom_call" | custom-call | flops 34500000 | tf_op jit(solution)/shard_map/conv_weight_grad/pallas_call | solution.py:54
  181.5 1.3 collective-permute-start.27
  183.2 3.3 %conv_weight_grad.5 = (bf16[4,64,1152]{2,1,0:T(8,128)(2,1)S(1)}, bf16[4,64,1152]{2,1,0:T(8,128)(2,1)S(1)}) custom-call(s32[2]{0:T(128)S(1)} %pad_add_fusion.refs_0_, bf16[3456,512]{1,0:T(8,128)(2,1)S(1)} %get-tuple-element.176.refs_1_, bf16[3456,512]{1,0:T(8,128)(2,1)S(1)} %get-tuple-element.177.refs_2_, bf16[3456,512]{1,0:T(8,128)(2,1)S(1)} %get-tuple-element.178.refs_3_, ...), custom_call_target="tpu_custom_call" | custom-call | flops 34500000 | tf_op jit(solution)/shard_map/conv_weight_grad/pallas_call | solution.py:54
  186.4 1.3 collective-permute-start.35
  188.6 4.2 %spread.8.refs_2_.refs_4_.refs_3_ = f32[128,768]{1,0:T(8,128)S(1)} custom-call(s32[2]{0:T(128)S(1)} %pad_add_fusion.refs_0_, s32[27,2048]{1,0:T(8,128)S(1)} %bitcast.49, bf16[3456,512]{1,0:T(8,128)(2,1)S(1)} %bitcast.39, bf16[512,512]{1,0:T(8,128)(2,1)S(1)} %collective-permute-done.20.refs_9_.refs_7_.refs_3_, ...), custom_call_target="tpu_custom_call" | custom-call | flops 1448999936 | tf_op jit(solution)/shard_map/spread/pallas_call | solution.py:54
  192.9 2.4 collective-permute-start.30
  195.7 4.4 %spread.9.refs_4_ = f32[128,768]{1,0:T(8,128)S(1)} custom-call(s32[2]{0:T(128)S(1)} %pad_add_fusion.refs_0_, s32[27,2048]{1,0:T(8,128)S(1)} %bitcast.50, bf16[3456,512]{1,0:T(8,128)(2,1)S(1)} %bitcast.40, bf16[512,512]{1,0:T(8,128)(2,1)S(1)} %collective-permute-done.20.refs_9_.refs_7_.refs_3_, f32[128,768]{1,0:T(8,128)S(1)} %spread.8.refs_2_.refs_4_.refs_3_, ...), custom_call_target="tpu_custom_call" | custom-call | flops 1448999936 | tf_op jit(solution)/shard_map/spread/pallas_call | solution.py:54
  200.1 4.2 %spread.10.refs_2_.refs_4_.refs_5_ = f32[128,768]{1,0:T(8,128)S(1)} custom-call(s32[2]{0:T(128)S(1)} %pad_add_fusion.refs_0_, s32[27,2048]{1,0:T(8,128)S(1)} %bitcast.51, bf16[3456,512]{1,0:T(8,128)(2,1)S(1)} %bitcast.41, bf16[512,512]{1,0:T(8,128)(2,1)S(1)} %collective-permute-done.21.refs_8_.refs_3_, f32[128,768]{1,0:T(8,128)S(1)} %spread.9.refs_4_), custom_call_target="tpu_custom_call" | custom-call | flops 1448999936 | tf_op jit(solution)/shard_map/spread/pallas_call | solution.py:54
  205.7 5.3 %collective-permute-start.36 = (bf16[512,512]{1,0:T(8,128)(2,1)S(1)}, bf16[512,512]{1,0:T(8,128)(2,1)S(1)}, u32[]{:S(2)}, u32[]{:S(2)}) collective-permute-start(bf16[512,512]{1,0:T(8,128)(2,1)S(1)} %collective-permute-done.35.refs_7_), channel_id=1, source_target_pairs={{0,1},{1,0},{2,3},{3,2},{4,5},{5,4},{6,7},{7,6},{8,9},{9,8},{10,11... | collective-permute-start | bytes 1572872 | tf_op jit(solution)/shard_map/ppermute | solution.py:1109
  211.0 4.2 %spread.11.refs_2_.refs_6_ = f32[128,768]{1,0:T(8,128)S(1)} custom-call(s32[2]{0:T(128)S(1)} %pad_add_fusion.refs_0_, s32[27,2048]{1,0:T(8,128)S(1)} %bitcast.52, bf16[3456,512]{1,0:T(8,128)(2,1)S(1)} %bitcast.42, bf16[512,512]{1,0:T(8,128)(2,1)S(1)} %collective-permute-done.21.refs_8_.refs_3_, f32[128,768]{1,0:T(8,128)S(1)} %spread.10.refs_2_.refs_4_.refs_5_, ...), custom_call_target="tpu_custom_call" | custom-call | flops 1448999936 | tf_op jit(solution)/shard_map/spread/pallas_call | solution.py:54
  216.3 1.8 collective-permute-start.34
  221.7 2.8 %collective-permute-done.37.refs_1_ = bf16[2,64,1152]{2,1,0:T(8,128)(2,1)S(1)} collective-permute-done((bf16[2,64,1152]{2,1,0:T(8,128)(2,1)S(1)}, bf16[2,64,1152]{2,1,0:T(8,128)(2,1)S(1)}, u32[]{:S(2)}, u32[]{:S(2)}) %collective-permute-start.37) | collective-permute-done | bytes 294944 | tf_op jit(solution)/shard_map/ppermute | solution.py:1109
  225.0 4.1 %collective-permute-start.32 = (bf16[128,256]{1,0:T(8,128)(2,1)S(1)}, bf16[128,256]{1,0:T(8,128)(2,1)S(1)}, u32[]{:S(2)}, u32[]{:S(2)}) collective-permute-start(bf16[128,256]{1,0:T(8,128)(2,1)S(1)} %get-tuple-element.211), channel_id=1, source_target_pairs={{0,4},{4,8},{8,12},{12,16},{16,20},{20,24},{24,28},{1,5},{5,9},{9,... | collective-permute-start | bytes 196616 | tf_op jit(solution)/shard_map/ppermute | solution.py:1281
  229.1 1.9 collective-permute-start.33
  231.6 10.7 %collective-permute-done.33.refs_3_ = bf16[128,256]{1,0:T(8,128)(2,1)S(1)} collective-permute-done((bf16[128,256]{1,0:T(8,128)(2,1)S(1)}, bf16[128,256]{1,0:T(8,128)(2,1)S(1)}, u32[]{:S(2)}, u32[]{:S(2)}) %collective-permute-start.33) | collective-permute-done | bytes 65568 | tf_op jit(solution)/shard_map/ppermute | solution.py:1280
  242.3 2.1 rows_out.1
  (97 shorter events, 20.9 us)
Async XLA Ops:
  1.5 6.3 %collective-permute-start.1 = (bf16[256,128]{1,0:T(8,128)(2,1)S(1)}, bf16[256,128]{1,0:T(8,128)(2,1)S(1)}, u32[]{:S(2)}, u32[]{:S(2)}) collective-permute-start(bf16[256,128]{1,0:T(8,128)(2,1)S(1)} %get-tuple-element.246), channel_id=1, source_target_pairs={{4,0},{8,4},{12,8},{16,12},{20,16},{24,20},{28,24},{5,1},{9,5},{13... | collective-permute-start | bytes 196616 | tf_op jit(solution)/shard_map/ppermute | solution.py:1159
  3.5 8.3 %collective-permute-start = (bf16[256,128]{1,0:T(8,128)(2,1)S(1)}, bf16[256,128]{1,0:T(8,128)(2,1)S(1)}, u32[]{:S(2)}, u32[]{:S(2)}) collective-permute-start(bf16[256,128]{1,0:T(8,128)(2,1)S(1)} %get-tuple-element.247), channel_id=1, source_target_pairs={{0,4},{4,8},{8,12},{12,16},{16,20},{20,24},{24,28},{1,5},{5,9},{9,... | collective-permute-start | bytes 196616 | tf_op jit(solution)/shard_map/ppermute | solution.py:1158
  7.8 3.9 %copy-start.1 = (s32[2048,27]{0,1:T(8,128)S(1)}, s32[2048,27]{0,1:T(8,128)}, u32[]{:S(2)}) copy-start(s32[2048,27]{0,1:T(8,128)} %param.23) | copy-start | bytes 663556
  7.8 3.9 %copy-start.2 = (bf16[2048,128]{1,0:T(8,128)(2,1)S(1)}, bf16[2048,128]{1,0:T(8,128)(2,1)}, u32[]{:S(2)}) copy-start(bf16[2048,128]{1,0:T(8,128)(2,1)} %refs_6_.4) | copy-start | bytes 1572868
  10.4 18.1 %collective-permute-start.8 = (bf16[784,512]{1,0:T(8,128)(2,1)S(1)}, bf16[784,512]{1,0:T(8,128)(2,1)S(1)}, u32[]{:S(2)}, u32[]{:S(2)}) collective-permute-start(bf16[784,512]{1,0:T(8,128)(2,1)S(1)} %get-tuple-element.143), channel_id=1, source_target_pairs={{0,2},{1,3},{2,0},{3,1},{4,6},{5,7},{6,4},{7,5},{8,10},{9,11},{10,... | collective-permute-start | bytes 2408456 | tf_op jit(solution)/shard_map/ppermute | solution.py:1109
  19.1 9.3 %collective-permute-start.4 = (bf16[256,512]{1,0:T(8,128)(2,1)S(1)}, bf16[256,512]{1,0:T(8,128)(2,1)S(1)}, u32[]{:S(2)}, u32[]{:S(2)}) collective-permute-start(bf16[256,512]{1,0:T(8,128)(2,1)S(1)} %get-tuple-element.133.refs_6_), channel_id=1, source_target_pairs={{0,1},{1,0},{2,3},{3,2},{4,5},{5,4},{6,7},{7,6},{8,9},{9,8},{10,11... | collective-permute-start | bytes 786440 | tf_op jit(solution)/shard_map/ppermute | solution.py:1109
  21.0 9.9 %collective-permute-start.5 = (bf16[256,512]{1,0:T(8,128)(2,1)S(1)}, bf16[256,512]{1,0:T(8,128)(2,1)S(1)}, u32[]{:S(2)}, u32[]{:S(2)}) collective-permute-start(bf16[256,512]{1,0:T(8,128)(2,1)S(1)} %get-tuple-element.140), channel_id=1, source_target_pairs={{0,1},{1,0},{2,3},{3,2},{4,5},{5,4},{6,7},{7,6},{8,9},{9,8},{10,11... | collective-permute-start | bytes 786440 | tf_op jit(solution)/shard_map/ppermute | solution.py:1109
  28.6 19.9 %collective-permute-start.9 = (bf16[784,512]{1,0:T(8,128)(2,1)S(1)}, bf16[784,512]{1,0:T(8,128)(2,1)S(1)}, u32[]{:S(2)}, u32[]{:S(2)}) collective-permute-start(bf16[784,512]{1,0:T(8,128)(2,1)S(1)} %collective-permute-done.8.refs_10_.refs_2_.refs_3_.refs_11_), channel_id=1, source_target_pairs={{0,1},{1,0},{2,3},{3,2},{4,5},{5,4},{6,7},{7,6},{8,9},{9,8},{10,11... | collective-permute-start | bytes 2408456 | tf_op jit(solution)/shard_map/ppermute | solution.py:1109
  30.9 17.5 %collective-permute-start.6 = (bf16[512,512]{1,0:T(8,128)(2,1)S(1)}, bf16[512,512]{1,0:T(8,128)(2,1)S(1)}, u32[]{:S(2)}, u32[]{:S(2)}) collective-permute-start(bf16[512,512]{1,0:T(8,128)(2,1)S(1)} %pad_maximum_fusion), channel_id=1, source_target_pairs={{0,2},{1,3},{2,0},{3,1},{4,6},{5,7},{6,4},{7,5},{8,10},{9,11},{10,... | collective-permute-start | bytes 1572872 | tf_op jit(solution)/shard_map/ppermute | solution.py:1109
  39.4 1.6 collective-permute-start.3
  39.7 8.7 %collective-permute-start.7 = (bf16[272,512]{1,0:T(8,128)(2,1)S(1)}, bf16[272,512]{1,0:T(8,128)(2,1)S(1)}, u32[]{:S(2)}, u32[]{:S(2)}) collective-permute-start(bf16[272,512]{1,0:T(8,128)(2,1)S(1)} %get-tuple-element.142), channel_id=1, source_target_pairs={{0,1},{1,0},{2,3},{3,2},{4,5},{5,4},{6,7},{7,6},{8,9},{9,8},{10,11... | collective-permute-start | bytes 835592 | tf_op jit(solution)/shard_map/ppermute | solution.py:1109
  40.0 8.4 %collective-permute-start.2 = (bf16[256,512]{1,0:T(8,128)(2,1)S(1)}, bf16[256,512]{1,0:T(8,128)(2,1)S(1)}, u32[]{:S(2)}, u32[]{:S(2)}) collective-permute-start(bf16[256,512]{1,0:T(8,128)(2,1)S(1)} %get-tuple-element.135.refs_6_), channel_id=1, source_target_pairs={{0,1},{1,0},{2,3},{3,2},{4,5},{5,4},{6,7},{7,6},{8,9},{9,8},{10,11... | collective-permute-start | bytes 786440 | tf_op jit(solution)/shard_map/ppermute | solution.py:1109
  40.2 8.2 %copy-start.3 = (bf16[128,512]{1,0:T(8,128)(2,1)S(1)}, bf16[128,512]{1,0:T(8,128)(2,1)}, u32[]{:S(2)}) copy-start(bf16[128,512]{1,0:T(8,128)(2,1)} %refs_9_.3) | copy-start | bytes 393220
  41.0 42.3 %collective-permute-start.13 = (bf16[1408,512]{1,0:T(8,128)(2,1)S(1)}, bf16[1408,512]{1,0:T(8,128)(2,1)S(1)}, u32[]{:S(2)}, u32[]{:S(2)}) collective-permute-start(bf16[1408,512]{1,0:T(8,128)(2,1)S(1)} %get-tuple-element.154), channel_id=1, source_target_pairs={{0,2},{1,3},{2,0},{3,1},{4,6},{5,7},{6,4},{7,5},{8,10},{9,11},{10,... | collective-permute-start | bytes 4325384 | tf_op jit(solution)/shard_map/ppermute | solution.py:1109
  50.2 2.2 collective-permute-start.10
  50.9 33.0 %collective-permute-start.12 = (bf16[1536,512]{1,0:T(8,128)(2,1)S(1)}, bf16[1536,512]{1,0:T(8,128)(2,1)S(1)}, u32[]{:S(2)}, u32[]{:S(2)}) collective-permute-start(bf16[1536,512]{1,0:T(8,128)(2,1)S(1)} %get-tuple-element.152), channel_id=1, source_target_pairs={{0,1},{1,0},{2,3},{3,2},{4,5},{5,4},{6,7},{7,6},{8,9},{9,8},{10,11... | collective-permute-start | bytes 4718600 | tf_op jit(solution)/shard_map/ppermute | solution.py:1109
  52.4 34.6 %copy-start.5 = (bf16[512,512]{1,0:T(8,128)(2,1)S(1)}, bf16[512,512]{1,0:T(8,128)(2,1)}, u32[]{:S(2)}) copy-start(bf16[512,512]{1,0:T(8,128)(2,1)} %refs_5_.1) | copy-start | bytes 1572868
  52.4 34.6 %copy-start.6 = (bf16[512,512]{1,0:T(8,128)(2,1)S(1)}, bf16[512,512]{1,0:T(8,128)(2,1)}, u32[]{:S(2)}) copy-start(bf16[512,512]{1,0:T(8,128)(2,1)} %refs_6_.5) | copy-start | bytes 1572868
  52.4 34.6 %copy-start.7 = (bf16[2048,128]{1,0:T(8,128)(2,1)S(1)}, bf16[2048,128]{1,0:T(8,128)(2,1)}, u32[]{:S(2)}) copy-start(bf16[2048,128]{1,0:T(8,128)(2,1)} %refs_4_.1) | copy-start | bytes 1572868
  52.4 34.6 %copy-start.8 = (bf16[128,512]{1,0:T(8,128)(2,1)S(1)}, bf16[128,512]{1,0:T(8,128)(2,1)}, u32[]{:S(2)}) copy-start(bf16[128,512]{1,0:T(8,128)(2,1)} %refs_7_.3) | copy-start | bytes 393220
  83.3 3.7 %collective-permute-start.14 = (bf16[1408,512]{1,0:T(8,128)(2,1)S(1)}, bf16[1408,512]{1,0:T(8,128)(2,1)S(1)}, u32[]{:S(2)}, u32[]{:S(2)}) collective-permute-start(bf16[1408,512]{1,0:T(8,128)(2,1)S(1)} %collective-permute-done.13.refs_13_), channel_id=1, source_target_pairs={{0,1},{1,0},{2,3},{3,2},{4,5},{5,4},{6,7},{7,6},{8,9},{9,8},{10,11... | collective-permute-start | bytes 4325384 | tf_op jit(solution)/shard_map/ppermute | solution.py:1109
  83.7 3.2 %collective-permute-start.11 = (bf16[256,512]{1,0:T(8,128)(2,1)S(1)}, bf16[256,512]{1,0:T(8,128)(2,1)S(1)}, u32[]{:S(2)}, u32[]{:S(2)}) collective-permute-start(bf16[256,512]{1,0:T(8,128)(2,1)S(1)} %get-tuple-element.150), channel_id=1, source_target_pairs={{0,1},{1,0},{2,3},{3,2},{4,5},{5,4},{6,7},{7,6},{8,9},{9,8},{10,11... | collective-permute-start | bytes 786440 | tf_op jit(solution)/shard_map/ppermute | solution.py:1109
  96.1 2.5 %collective-permute-start.15 = (bf16[256,512]{1,0:T(8,128)(2,1)S(1)}, bf16[256,512]{1,0:T(8,128)(2,1)S(1)}, u32[]{:S(2)}, u32[]{:S(2)}) collective-permute-start(bf16[256,512]{1,0:T(8,128)(2,1)S(1)} %get-tuple-element.157), channel_id=1, source_target_pairs={{0,1},{1,0},{2,3},{3,2},{4,5},{5,4},{6,7},{7,6},{8,9},{9,8},{10,11... | collective-permute-start | bytes 786440 | tf_op jit(solution)/shard_map/ppermute | solution.py:1109
  98.7 19.4 %collective-permute-start.16 = (bf16[2,8,64,1152]{3,2,1,0:T(8,128)(2,1)S(1)}, bf16[2,8,64,1152]{3,2,1,0:T(8,128)(2,1)S(1)}, u32[]{:S(2)}, u32[]{:S(2)}) collective-permute-start(bf16[2,8,64,1152]{3,2,1,0:T(8,128)(2,1)S(1)} %second_send.1.refs_6_), channel_id=1, source_target_pairs={{0,1},{1,0},{2,3},{3,2},{4,5},{5,4},{6,7},{7,6},{8,9},{9,8},{10,11... | collective-permute-start | bytes 7077896 | tf_op jit(solution)/shard_map/ppermute | solution.py:1109
  120.2 27.2 %collective-permute-start.18 = (bf16[8,64,1152]{2,1,0:T(8,128)(2,1)S(1)}, bf16[8,64,1152]{2,1,0:T(8,128)(2,1)S(1)}, u32[]{:S(2)}, u32[]{:S(2)}) collective-permute-start(bf16[8,64,1152]{2,1,0:T(8,128)(2,1)S(1)} %get-tuple-element.175), channel_id=1, source_target_pairs={{0,2},{1,3},{2,0},{3,1},{4,6},{5,7},{6,4},{7,5},{8,10},{9,11},{10,... | collective-permute-start | bytes 3538952 | tf_op jit(solution)/shard_map/ppermute | solution.py:1109
  142.1 2.3 collective-permute-start.17
  146.8 13.2 %collective-permute-start.20 = (bf16[512,512]{1,0:T(8,128)(2,1)S(1)}, bf16[512,512]{1,0:T(8,128)(2,1)S(1)}, u32[]{:S(2)}, u32[]{:S(2)}) collective-permute-start(bf16[512,512]{1,0:T(8,128)(2,1)S(1)} %get-tuple-element.174.refs_3_.refs_5_), channel_id=1, source_target_pairs={{0,2},{1,3},{2,0},{3,1},{4,6},{5,7},{6,4},{7,5},{8,10},{9,11},{10,... | collective-permute-start | bytes 1572872 | tf_op jit(solution)/shard_map/ppermute | solution.py:1109
  147.7 13.7 %collective-permute-start.23 = (bf16[4,64,1152]{2,1,0:T(8,128)(2,1)S(1)}, bf16[4,64,1152]{2,1,0:T(8,128)(2,1)S(1)}, u32[]{:S(2)}, u32[]{:S(2)}) collective-permute-start(bf16[4,64,1152]{2,1,0:T(8,128)(2,1)S(1)} %get-tuple-element.189), channel_id=1, source_target_pairs={{0,4},{4,0},{8,12},{12,8},{16,20},{20,16},{24,28},{28,24},{1,5},{5... | collective-permute-start | bytes 1769480 | tf_op jit(solution)/shard_map/ppermute | solution.py:1109
  156.4 4.8 %collective-permute-start.22 = (bf16[2,8,80,128]{3,2,1,0:T(8,128)(2,1)S(1)}, bf16[2,8,80,128]{3,2,1,0:T(8,128)(2,1)S(1)}, u32[]{:S(2)}, u32[]{:S(2)}) collective-permute-start(bf16[2,8,80,128]{3,2,1,0:T(8,128)(2,1)S(1)} %get-tuple-element.185), channel_id=1, source_target_pairs={{0,1},{1,0},{2,3},{3,2},{4,5},{5,4},{6,7},{7,6},{8,9},{9,8},{10,11... | collective-permute-start | bytes 983048 | tf_op jit(solution)/shard_map/ppermute | solution.py:1109
  157.7 6.8 %collective-permute-start.19 = (bf16[512,512]{1,0:T(8,128)(2,1)S(1)}, bf16[512,512]{1,0:T(8,128)(2,1)S(1)}, u32[]{:S(2)}, u32[]{:S(2)}) collective-permute-start(bf16[512,512]{1,0:T(8,128)(2,1)S(1)} %get-tuple-element.174.refs_3_.refs_5_), channel_id=1, source_target_pairs={{0,1},{1,0},{2,3},{3,2},{4,5},{5,4},{6,7},{7,6},{8,9},{9,8},{10,11... | collective-permute-start | bytes 1572872 | tf_op jit(solution)/shard_map/ppermute | solution.py:1109
  160.0 4.5 %collective-permute-start.21 = (bf16[512,512]{1,0:T(8,128)(2,1)S(1)}, bf16[512,512]{1,0:T(8,128)(2,1)S(1)}, u32[]{:S(2)}, u32[]{:S(2)}) collective-permute-start(bf16[512,512]{1,0:T(8,128)(2,1)S(1)} %collective-permute-done.20.refs_9_.refs_7_.refs_3_), channel_id=1, source_target_pairs={{0,1},{1,0},{2,3},{3,2},{4,5},{5,4},{6,7},{7,6},{8,9},{9,8},{10,11... | collective-permute-start | bytes 1572872 | tf_op jit(solution)/shard_map/ppermute | solution.py:1109
  163.2 14.2 %collective-permute-start.24 = (bf16[8,64,640]{2,1,0:T(8,128)(2,1)S(1)}, bf16[8,64,640]{2,1,0:T(8,128)(2,1)S(1)}, u32[]{:S(2)}, u32[]{:S(2)}) collective-permute-start(bf16[8,64,640]{2,1,0:T(8,128)(2,1)S(1)} %get-tuple-element.195), channel_id=1, source_target_pairs={{0,2},{1,3},{2,0},{3,1},{4,6},{5,7},{6,4},{7,5},{8,10},{9,11},{10,... | collective-permute-start | bytes 1966088 | tf_op jit(solution)/shard_map/ppermute | solution.py:1109
  167.8 15.0 %collective-permute-start.25 = (bf16[4,64,1152]{2,1,0:T(8,128)(2,1)S(1)}, bf16[4,64,1152]{2,1,0:T(8,128)(2,1)S(1)}, u32[]{:S(2)}, u32[]{:S(2)}) collective-permute-start(bf16[4,64,1152]{2,1,0:T(8,128)(2,1)S(1)} %get-tuple-element.197), channel_id=1, source_target_pairs={{0,4},{4,0},{8,12},{12,8},{16,20},{20,16},{24,28},{28,24},{1,5},{5... | collective-permute-start | bytes 1769480 | tf_op jit(solution)/shard_map/ppermute | solution.py:1109
  180.8 23.6 %collective-permute-start.28 = (bf16[4,64,1792]{2,1,0:T(8,128)(2,1)S(1)}, bf16[4,64,1792]{2,1,0:T(8,128)(2,1)S(1)}, u32[]{:S(2)}, u32[]{:S(2)}) collective-permute-start(bf16[4,64,1792]{2,1,0:T(8,128)(2,1)S(1)} %get-tuple-element.204), channel_id=1, source_target_pairs={{0,4},{4,0},{8,12},{12,8},{16,20},{20,16},{24,28},{28,24},{1,5},{5... | collective-permute-start | bytes 2752520 | tf_op jit(solution)/shard_map/ppermute | solution.py:1109
  181.5 11.4 %collective-permute-start.27 = (bf16[2,64,1152]{2,1,0:T(8,128)(2,1)S(1)}, bf16[2,64,1152]{2,1,0:T(8,128)(2,1)S(1)}, u32[]{:S(2)}, u32[]{:S(2)}) collective-permute-start(bf16[2,64,1152]{2,1,0:T(8,128)(2,1)S(1)} %get-tuple-element.193.refs_5_), channel_id=1, source_target_pairs={{0,8},{4,12},{8,0},{12,4},{16,24},{20,28},{24,16},{28,20},{1,9},{5... | collective-permute-start | bytes 884744 | tf_op jit(solution)/shard_map/ppermute | solution.py:1109
  182.9 12.3 %collective-permute-start.26 = (bf16[2,64,1152]{2,1,0:T(8,128)(2,1)S(1)}, bf16[2,64,1152]{2,1,0:T(8,128)(2,1)S(1)}, u32[]{:S(2)}, u32[]{:S(2)}) collective-permute-start(bf16[2,64,1152]{2,1,0:T(8,128)(2,1)S(1)} %get-tuple-element.198.refs_10_), channel_id=1, source_target_pairs={{0,8},{4,12},{8,0},{12,4},{16,24},{20,28},{24,16},{28,20},{1,9},{5... | collective-permute-start | bytes 884744 | tf_op jit(solution)/shard_map/ppermute | solution.py:1109
  186.4 19.3 %collective-permute-start.35 = (bf16[512,512]{1,0:T(8,128)(2,1)S(1)}, bf16[512,512]{1,0:T(8,128)(2,1)S(1)}, u32[]{:S(2)}, u32[]{:S(2)}) collective-permute-start(bf16[512,512]{1,0:T(8,128)(2,1)S(1)} %get-tuple-element.218), channel_id=1, source_target_pairs={{0,2},{1,3},{2,0},{3,1},{4,6},{5,7},{6,4},{7,5},{8,10},{9,11},{10,... | collective-permute-start | bytes 1572872 | tf_op jit(solution)/shard_map/ppermute | solution.py:1109
  187.7 27.5 %collective-permute-start.31 = (bf16[4,64,1152]{2,1,0:T(8,128)(2,1)S(1)}, bf16[4,64,1152]{2,1,0:T(8,128)(2,1)S(1)}, u32[]{:S(2)}, u32[]{:S(2)}) collective-permute-start(bf16[4,64,1152]{2,1,0:T(8,128)(2,1)S(1)} %get-tuple-element.206), channel_id=1, source_target_pairs={{0,4},{4,0},{8,12},{12,8},{16,20},{20,16},{24,28},{28,24},{1,5},{5... | collective-permute-start | bytes 1769480 | tf_op jit(solution)/shard_map/ppermute | solution.py:1109
  192.9 18.1 %collective-permute-start.30 = (bf16[1,64,1152]{2,1,0:T(8,128)(2,1)S(1)}, bf16[1,64,1152]{2,1,0:T(8,128)(2,1)S(1)}, u32[]{:S(2)}, u32[]{:S(2)}) collective-permute-start(bf16[1,64,1152]{2,1,0:T(8,128)(2,1)S(1)} %get-tuple-element.203.refs_6_), channel_id=1, source_target_pairs={{0,16},{4,20},{8,24},{12,28},{16,0},{20,4},{24,8},{28,12},{1,17},{... | collective-permute-start | bytes 442376 | tf_op jit(solution)/shard_map/ppermute | solution.py:1109
  195.4 15.7 %collective-permute-start.29 = (bf16[1,64,1152]{2,1,0:T(8,128)(2,1)S(1)}, bf16[1,64,1152]{2,1,0:T(8,128)(2,1)S(1)}, u32[]{:S(2)}, u32[]{:S(2)}) collective-permute-start(bf16[1,64,1152]{2,1,0:T(8,128)(2,1)S(1)} %get-tuple-element.201.refs_5_), channel_id=1, source_target_pairs={{0,16},{4,20},{8,24},{12,28},{16,0},{20,4},{24,8},{28,12},{1,17},{... | collective-permute-start | bytes 442376 | tf_op jit(solution)/shard_map/ppermute | solution.py:1109
  204.6 16.1 %collective-permute-start.38 = (bf16[2,64,1792]{2,1,0:T(8,128)(2,1)S(1)}, bf16[2,64,1792]{2,1,0:T(8,128)(2,1)S(1)}, u32[]{:S(2)}, u32[]{:S(2)}) collective-permute-start(bf16[2,64,1792]{2,1,0:T(8,128)(2,1)S(1)} %get-tuple-element.205.refs_5_), channel_id=1, source_target_pairs={{0,8},{4,12},{8,0},{12,4},{16,24},{20,28},{24,16},{28,20},{1,9},{5... | collective-permute-start | bytes 1376264 | tf_op jit(solution)/shard_map/ppermute | solution.py:1109
  205.7 36.6 %collective-permute-start.36 = (bf16[512,512]{1,0:T(8,128)(2,1)S(1)}, bf16[512,512]{1,0:T(8,128)(2,1)S(1)}, u32[]{:S(2)}, u32[]{:S(2)}) collective-permute-start(bf16[512,512]{1,0:T(8,128)(2,1)S(1)} %collective-permute-done.35.refs_7_), channel_id=1, source_target_pairs={{0,1},{1,0},{2,3},{3,2},{4,5},{5,4},{6,7},{7,6},{8,9},{9,8},{10,11... | collective-permute-start | bytes 1572872 | tf_op jit(solution)/shard_map/ppermute | solution.py:1109
  215.4 9.2 %collective-permute-start.37 = (bf16[2,64,1152]{2,1,0:T(8,128)(2,1)S(1)}, bf16[2,64,1152]{2,1,0:T(8,128)(2,1)S(1)}, u32[]{:S(2)}, u32[]{:S(2)}) collective-permute-start(bf16[2,64,1152]{2,1,0:T(8,128)(2,1)S(1)} %get-tuple-element.207.refs_7_), channel_id=1, source_target_pairs={{0,8},{4,12},{8,0},{12,4},{16,24},{20,28},{24,16},{28,20},{1,9},{5... | collective-permute-start | bytes 884744 | tf_op jit(solution)/shard_map/ppermute | solution.py:1109
  216.3 12.8 %collective-permute-start.34 = (bf16[512,256]{1,0:T(8,128)(2,1)S(1)}, bf16[512,256]{1,0:T(8,128)(2,1)S(1)}, u32[]{:S(2)}, u32[]{:S(2)}) collective-permute-start(bf16[512,256]{1,0:T(8,128)(2,1)S(1)} %get-tuple-element.216), channel_id=1, source_target_pairs={{0,1},{1,0},{2,3},{3,2},{4,5},{5,4},{6,7},{7,6},{8,9},{9,8},{10,11... | collective-permute-start | bytes 786440 | tf_op jit(solution)/shard_map/ppermute | solution.py:1109
  220.9 23.6 %collective-permute-start.39 = (bf16[1,64,1792]{2,1,0:T(8,128)(2,1)S(1)}, bf16[1,64,1792]{2,1,0:T(8,128)(2,1)S(1)}, u32[]{:S(2)}, u32[]{:S(2)}) collective-permute-start(bf16[1,64,1792]{2,1,0:T(8,128)(2,1)S(1)} %get-tuple-element.222.refs_2_), channel_id=1, source_target_pairs={{0,16},{4,20},{8,24},{12,28},{16,0},{20,4},{24,8},{28,12},{1,17},{... | collective-permute-start | bytes 688136 | tf_op jit(solution)/shard_map/ppermute | solution.py:1109
  224.7 19.8 %collective-permute-start.40 = (bf16[1,64,1152]{2,1,0:T(8,128)(2,1)S(1)}, bf16[1,64,1152]{2,1,0:T(8,128)(2,1)S(1)}, u32[]{:S(2)}, u32[]{:S(2)}) collective-permute-start(bf16[1,64,1152]{2,1,0:T(8,128)(2,1)S(1)} %get-tuple-element.223.refs_9_), channel_id=1, source_target_pairs={{0,16},{4,20},{8,24},{12,28},{16,0},{20,4},{24,8},{28,12},{1,17},{... | collective-permute-start | bytes 442376 | tf_op jit(solution)/shard_map/ppermute | solution.py:1109
  225.0 6.6 %collective-permute-start.32 = (bf16[128,256]{1,0:T(8,128)(2,1)S(1)}, bf16[128,256]{1,0:T(8,128)(2,1)S(1)}, u32[]{:S(2)}, u32[]{:S(2)}) collective-permute-start(bf16[128,256]{1,0:T(8,128)(2,1)S(1)} %get-tuple-element.211), channel_id=1, source_target_pairs={{0,4},{4,8},{8,12},{12,16},{16,20},{20,24},{24,28},{1,5},{5,9},{9,... | collective-permute-start | bytes 196616 | tf_op jit(solution)/shard_map/ppermute | solution.py:1281
  229.1 13.2 %collective-permute-start.33 = (bf16[128,256]{1,0:T(8,128)(2,1)S(1)}, bf16[128,256]{1,0:T(8,128)(2,1)S(1)}, u32[]{:S(2)}, u32[]{:S(2)}) collective-permute-start(bf16[128,256]{1,0:T(8,128)(2,1)S(1)} %get-tuple-element.212), channel_id=1, source_target_pairs={{4,0},{8,4},{12,8},{16,12},{20,16},{24,20},{28,24},{5,1},{9,5},{13... | collective-permute-start | bytes 196616 | tf_op jit(solution)/shard_map/ppermute | solution.py:1280
  (2 other events, 4.8 us)
